TPU v7x, 256 devices: a whole 4x4x8 slice. The times are simulated.
256 devices in a mesh: dom: 64 (over z, y, core), rows: 4 (over x).
Axes of the slice: x: 4, y: 4, z: 8, core: 2. Of those that a mesh axis runs over, the one named last changes fastest.
Arguments:
- images: bfloat16 [28672, 25600], P('dom', 'rows'), may hold values from -6 to 6
- panels: bfloat16 [128, 25600, 256], P('dom', 'rows')
- mean_panels: float32 [128, 25600], P('dom', 'rows'), may hold values from -6 to 6
- ctf_table: float32 [16, 25600], P(None, 'rows'), may hold values from -1 to 1
- pose_bin: int32 [28672], P('dom'), may hold values from 0 to 1
- ctf_group: int32 [28672], P('dom'), may hold values from 0 to 15
Outputs:
- scores: float32 [28672, 256], P('dom')
- factor: float32 [256, 256], replicated
All inputs are finite; a program needn't handle non-finite values.
Results may differ from a plain program's by a relative error of at most 0.003.
Values sent between devices are 32-bit elements; how exact they have to be, the bound alone decides.
No kernel may reach another device: no remote copies, remote signals or barrier semaphores. Data moves between devices by JAX's collectives and lax.ppermute only.
A program may use at most 128 MiB of HBM per device.

v0:
```python
import jax
import jax.numpy as jnp
from jax import lax
from jax.sharding import PartitionSpec as P


def high_dot(left, right):
    return jnp.dot(left, right, precision=lax.Precision.HIGHEST, preferred_element_type=jnp.float32)


def cholesky_small(matrix):
    order = matrix.shape[0]
    places = jnp.arange(order, dtype=jnp.int32)

    def column_step(index, carry):
        work, lower = carry
        index = jnp.asarray(index).astype(jnp.int32)
        column = lax.dynamic_slice_in_dim(work, index, 1, 1)[:, 0]
        pivot = jnp.sqrt(lax.dynamic_slice_in_dim(column, index, 1, 0)[0])
        below = jnp.where(places > index, column / pivot, jnp.zeros_like(column))
        filled = below + jnp.where(places == index, pivot, jnp.zeros_like(column))
        lower = lower + filled[:, None] * (places == index).astype(matrix.dtype)[None, :]
        work = work - below[:, None] * below[None, :]
        return (work, lower)

    return lax.fori_loop(0, order, column_step, (matrix, jnp.zeros_like(matrix)))[1]


def inverse_small(lower):
    order = lower.shape[0]
    places = jnp.arange(order, dtype=jnp.int32)

    def row_step(index, inverse):
        index = jnp.asarray(index).astype(jnp.int32)
        row_lower = lax.dynamic_slice_in_dim(lower, index, 1, 0)[0]
        pivot = lax.dynamic_slice_in_dim(row_lower, index, 1, 0)[0]
        unit = (places == index).astype(lower.dtype)
        solved = (unit - high_dot(row_lower, inverse)) / pivot
        return inverse + unit[:, None] * solved[None, :]

    return lax.fori_loop(0, order, row_step, jnp.zeros_like(lower))


def assemble(top_left, bottom_left, bottom_right):
    half = top_left.shape[0]
    rest = bottom_right.shape[0]
    upper_part = jnp.concatenate([top_left, jnp.zeros((half, rest), top_left.dtype)], axis=1)
    lower_part = jnp.concatenate([bottom_left, bottom_right], axis=1)
    return jnp.concatenate([upper_part, lower_part], axis=0)


def cholesky_pair(matrix):
    order = matrix.shape[0]
    if order <= 16:
        lower = cholesky_small(matrix)
        return (lower, inverse_small(lower))
    half = order // 2
    lower_a, inverse_a = cholesky_pair(matrix[:half, :half])
    below = high_dot(matrix[half:, :half], inverse_a.T)
    schur = matrix[half:, half:] - high_dot(below, below.T)
    lower_b, inverse_b = cholesky_pair(schur)
    inverse_mid = -high_dot(inverse_b, high_dot(below, inverse_a))
    return (assemble(lower_a, below, lower_b), assemble(inverse_a, inverse_mid, inverse_b))


def weighted_rows(images, pose_bin, ctf_group, mean_panels, ctf_table):
    ctf_rows = jnp.take(ctf_table, ctf_group, axis=0)
    mean_rows = jnp.broadcast_to(mean_panels[0][None, :], images.shape)
    mean_rows = jnp.where((pose_bin == 1)[:, None], mean_panels[1][None, :], mean_rows)
    return (ctf_rows * (images.astype(jnp.float32) - ctf_rows * mean_rows)).astype(jnp.bfloat16)


def project(weighted, pose_bin, panels):
    coeffs = jnp.zeros((weighted.shape[0], panels.shape[2]), jnp.float32)
    for which in range(panels.shape[0]):
        chosen = jnp.where((pose_bin == which)[:, None], weighted, jnp.zeros_like(weighted))
        coeffs = coeffs + jnp.dot(chosen, panels[which], preferred_element_type=jnp.float32)
    return coeffs


def gram_of(coeffs):
    return high_dot(coeffs.T, coeffs)


def body(images, panels, mean_panels, ctf_table, pose_bin, ctf_group):
    weighted = weighted_rows(images, pose_bin, ctf_group, mean_panels, ctf_table)
    particles = images.shape[0] * lax.axis_size("dom")
    coeffs = lax.psum(project(weighted, pose_bin, panels), "rows")
    gram = gram_of(coeffs)
    gram = gram / particles
    lower, inverse = cholesky_pair(lax.psum(gram, "dom"))
    factor = lower.T
    scores = jnp.dot(coeffs, inverse.T, precision=lax.Precision.HIGHEST)
    return (scores, factor)


def solution(mesh):
    placed = (
        P("dom", "rows"),
        P("dom", "rows", None),
        P("dom", "rows"),
        P(None, "rows"),
        P("dom"),
        P("dom"),
    )
    return jax.shard_map(
        body, mesh=mesh, in_specs=placed, out_specs=(P("dom", None), P()), check_vma=False
    )
```

profile of v0, /device:TPU:1, one launch (start us, length us, event | category | flops | bytes accessed | tf_op | source)
XLA Modules:
  0.0 1036.6 jit_solution(16487849600302292316)
XLA Ops:
  28.9 49.3 %all-reduce.33.cloned.1.call-done = f32[448,256]{1,0:T(8,128)} async-done(((f32[448,256]{1,0:T(8,128)}), f32[448,256]{1,0:T(8,128)}) %all-reduce.33.cloned.1.call-update) | async-done | bytes 458768 | tf_op jit(solution)/shard_map/psum | solution.py:88
  81.4 179.2 %all-reduce.35.cloned.1.call-done = f32[256,256]{1,0:T(8,128)} async-done(((f32[256,256]{1,0:T(8,128)}), f32[256,256]{1,0:T(8,128)}) %all-reduce.35.cloned.1.call-update) | async-done | bytes 262160 | tf_op jit(solution)/shard_map/psum | solution.py:91
  261.4 23.6 %while.608 = (s32[]{:T(128)}, f32[16,16]{0,1:T(8,128)S(1)}, f32[16,16]{1,0:T(8,128)S(1)}, s32[]{:T(128)}, s32[]{:T(128)}, /*index=5*/s32[]{:T(128)}) while((s32[]{:T(128)}, f32[16,16]{0,1:T(8,128)S(1)}, f32[16,16]{1,0:T(8,128)S(1)}, s32[]{:T(128)}, s32[]{:T(128)}, /*index=5*/s32[]{:T(128)}) %tuple.1341), condition=%wide.region_3.4_spmd.clone.clone, body=%wide.region_2.3_spmd.clone.clone.sunk | while | flops 1476 | bytes 7039 | solution.py:26
  310.1 23.6 %while.609 = (s32[]{:T(128)}, f32[16,16]{0,1:T(8,128)S(1)}, f32[16,16]{1,0:T(8,128)S(1)}, s32[]{:T(128)}, s32[]{:T(128)}, /*index=5*/s32[]{:T(128)}) while((s32[]{:T(128)}, f32[16,16]{0,1:T(8,128)S(1)}, f32[16,16]{1,0:T(8,128)S(1)}, s32[]{:T(128)}, s32[]{:T(128)}, /*index=5*/s32[]{:T(128)}) %tuple.1347), condition=%wide.region_7.8_spmd.clone.clone, body=%wide.region_6.7_spmd.clone.clone.sunk | while | flops 1476 | bytes 7039 | solution.py:26
  359.2 23.6 %while.610 = (s32[]{:T(128)}, f32[16,16]{0,1:T(8,128)S(1)}, f32[16,16]{1,0:T(8,128)S(1)}, s32[]{:T(128)}, s32[]{:T(128)}, /*index=5*/s32[]{:T(128)}) while((s32[]{:T(128)}, f32[16,16]{0,1:T(8,128)S(1)}, f32[16,16]{1,0:T(8,128)S(1)}, s32[]{:T(128)}, s32[]{:T(128)}, /*index=5*/s32[]{:T(128)}) %tuple.1353), condition=%wide.region_11.12_spmd.clone.clone, body=%wide.region_10.11_spmd.clone.clone.sunk | while | flops 1476 | bytes 7039 | solution.py:26
  382.8 23.2 %while.594 = (s32[]{:T(128)}, f32[16,16]{1,0:T(8,128)S(1)}, f32[16,16]{1,0:T(8,128)S(1)}, s32[]{:T(128)}, s32[]{:T(128)}, /*index=5*/s32[]{:T(128)}) while((s32[]{:T(128)}, f32[16,16]{1,0:T(8,128)S(1)}, f32[16,16]{1,0:T(8,128)S(1)}, s32[]{:T(128)}, s32[]{:T(128)}, /*index=5*/s32[]{:T(128)}) %tuple.1356), condition=%wide.region_13.14_spmd.clone, body=%wide.region_12.13_spmd.clone.sunk | while | flops 4196 | bytes 12656 | solution.py:41
  406.5 23.6 %while.611 = (s32[]{:T(128)}, f32[16,16]{0,1:T(8,128)S(1)}, f32[16,16]{1,0:T(8,128)S(1)}, s32[]{:T(128)}, s32[]{:T(128)}, /*index=5*/s32[]{:T(128)}) while((s32[]{:T(128)}, f32[16,16]{0,1:T(8,128)S(1)}, f32[16,16]{1,0:T(8,128)S(1)}, s32[]{:T(128)}, s32[]{:T(128)}, /*index=5*/s32[]{:T(128)}) %tuple.1359), condition=%wide.region_15.16_spmd.clone.clone, body=%wide.region_14.15_spmd.clone.clone.sunk | while | flops 1476 | bytes 7039 | solution.py:26
  430.2 23.2 %while.595 = (s32[]{:T(128)}, f32[16,16]{1,0:T(8,128)S(1)}, f32[16,16]{1,0:T(8,128)S(1)}, s32[]{:T(128)}, s32[]{:T(128)}, /*index=5*/s32[]{:T(128)}) while((s32[]{:T(128)}, f32[16,16]{1,0:T(8,128)S(1)}, f32[16,16]{1,0:T(8,128)S(1)}, s32[]{:T(128)}, s32[]{:T(128)}, /*index=5*/s32[]{:T(128)}) %tuple.1362), condition=%wide.region_17.18_spmd.clone, body=%wide.region_16.17_spmd.clone.sunk | while | flops 4196 | bytes 12656 | solution.py:41
  455.8 23.6 %while.612 = (s32[]{:T(128)}, f32[16,16]{0,1:T(8,128)S(1)}, f32[16,16]{1,0:T(8,128)S(1)}, s32[]{:T(128)}, s32[]{:T(128)}, /*index=5*/s32[]{:T(128)}) while((s32[]{:T(128)}, f32[16,16]{0,1:T(8,128)S(1)}, f32[16,16]{1,0:T(8,128)S(1)}, s32[]{:T(128)}, s32[]{:T(128)}, /*index=5*/s32[]{:T(128)}) %tuple.1365), condition=%wide.region_19.20_spmd.clone.clone, body=%wide.region_18.19_spmd.clone.clone.sunk | while | flops 1476 | bytes 7039 | solution.py:26
  503.3 23.6 %while.613 = (s32[]{:T(128)}, f32[16,16]{0,1:T(8,128)S(1)}, f32[16,16]{1,0:T(8,128)S(1)}, s32[]{:T(128)}, s32[]{:T(128)}, /*index=5*/s32[]{:T(128)}) while((s32[]{:T(128)}, f32[16,16]{0,1:T(8,128)S(1)}, f32[16,16]{1,0:T(8,128)S(1)}, s32[]{:T(128)}, s32[]{:T(128)}, /*index=5*/s32[]{:T(128)}) %tuple.1371), condition=%wide.region_23.24_spmd.clone.clone, body=%wide.region_22.23_spmd.clone.clone.sunk | while | flops 1476 | bytes 7039 | solution.py:26
  551.0 23.6 %while.614 = (s32[]{:T(128)}, f32[16,16]{0,1:T(8,128)S(1)}, f32[16,16]{1,0:T(8,128)S(1)}, s32[]{:T(128)}, s32[]{:T(128)}, /*index=5*/s32[]{:T(128)}) while((s32[]{:T(128)}, f32[16,16]{0,1:T(8,128)S(1)}, f32[16,16]{1,0:T(8,128)S(1)}, s32[]{:T(128)}, s32[]{:T(128)}, /*index=5*/s32[]{:T(128)}) %tuple.1377), condition=%wide.region_27.28_spmd.clone.clone, body=%wide.region_26.27_spmd.clone.clone.sunk | while | flops 1476 | bytes 7039 | solution.py:26
  598.4 23.6 %while.615 = (s32[]{:T(128)}, f32[16,16]{0,1:T(8,128)S(1)}, f32[16,16]{1,0:T(8,128)S(1)}, s32[]{:T(128)}, s32[]{:T(128)}, /*index=5*/s32[]{:T(128)}) while((s32[]{:T(128)}, f32[16,16]{0,1:T(8,128)S(1)}, f32[16,16]{1,0:T(8,128)S(1)}, s32[]{:T(128)}, s32[]{:T(128)}, /*index=5*/s32[]{:T(128)}) %tuple.1383), condition=%wide.region_31.32_spmd.clone.clone, body=%wide.region_30.31_spmd.clone.clone.sunk | while | flops 1476 | bytes 7039 | solution.py:26
  646.5 23.6 %while.616 = (s32[]{:T(128)}, f32[16,16]{0,1:T(8,128)S(1)}, f32[16,16]{1,0:T(8,128)S(1)}, s32[]{:T(128)}, s32[]{:T(128)}, /*index=5*/s32[]{:T(128)}) while((s32[]{:T(128)}, f32[16,16]{0,1:T(8,128)S(1)}, f32[16,16]{1,0:T(8,128)S(1)}, s32[]{:T(128)}, s32[]{:T(128)}, /*index=5*/s32[]{:T(128)}) %tuple.1389), condition=%wide.region_35.36_spmd.clone.clone, body=%wide.region_34.35_spmd.clone.clone.sunk | while | flops 1476 | bytes 7039 | solution.py:26
  670.1 23.2 %while.600 = (s32[]{:T(128)}, f32[16,16]{1,0:T(8,128)S(1)}, f32[16,16]{1,0:T(8,128)S(1)}, s32[]{:T(128)}, s32[]{:T(128)}, /*index=5*/s32[]{:T(128)}) while((s32[]{:T(128)}, f32[16,16]{1,0:T(8,128)S(1)}, f32[16,16]{1,0:T(8,128)S(1)}, s32[]{:T(128)}, s32[]{:T(128)}, /*index=5*/s32[]{:T(128)}) %tuple.1392), condition=%wide.region_37.38_spmd.clone, body=%wide.region_36.37_spmd.clone.sunk | while | flops 4196 | bytes 12656 | solution.py:41
  693.8 23.6 %while.617 = (s32[]{:T(128)}, f32[16,16]{0,1:T(8,128)S(1)}, f32[16,16]{1,0:T(8,128)S(1)}, s32[]{:T(128)}, s32[]{:T(128)}, /*index=5*/s32[]{:T(128)}) while((s32[]{:T(128)}, f32[16,16]{0,1:T(8,128)S(1)}, f32[16,16]{1,0:T(8,128)S(1)}, s32[]{:T(128)}, s32[]{:T(128)}, /*index=5*/s32[]{:T(128)}) %tuple.1395), condition=%wide.region_39.40_spmd.clone.clone, body=%wide.region_38.39_spmd.clone.clone.sunk | while | flops 1476 | bytes 7039 | solution.py:26
  717.5 23.2 %while.601 = (s32[]{:T(128)}, f32[16,16]{1,0:T(8,128)S(1)}, f32[16,16]{1,0:T(8,128)S(1)}, s32[]{:T(128)}, s32[]{:T(128)}, /*index=5*/s32[]{:T(128)}) while((s32[]{:T(128)}, f32[16,16]{1,0:T(8,128)S(1)}, f32[16,16]{1,0:T(8,128)S(1)}, s32[]{:T(128)}, s32[]{:T(128)}, /*index=5*/s32[]{:T(128)}) %tuple.1398), condition=%wide.region_41.42_spmd.clone, body=%wide.region_40.41_spmd.clone.sunk | while | flops 4196 | bytes 12656 | solution.py:41
  741.5 23.6 %while.618 = (s32[]{:T(128)}, f32[16,16]{0,1:T(8,128)S(1)}, f32[16,16]{1,0:T(8,128)S(1)}, s32[]{:T(128)}, s32[]{:T(128)}, /*index=5*/s32[]{:T(128)}) while((s32[]{:T(128)}, f32[16,16]{0,1:T(8,128)S(1)}, f32[16,16]{1,0:T(8,128)S(1)}, s32[]{:T(128)}, s32[]{:T(128)}, /*index=5*/s32[]{:T(128)}) %tuple.1401), condition=%wide.region_43.44_spmd.clone.clone, body=%wide.region_42.43_spmd.clone.clone.sunk | while | flops 1476 | bytes 7039 | solution.py:26
  788.9 23.6 %while.619 = (s32[]{:T(128)}, f32[16,16]{0,1:T(8,128)S(1)}, f32[16,16]{1,0:T(8,128)S(1)}, s32[]{:T(128)}, s32[]{:T(128)}, /*index=5*/s32[]{:T(128)}) while((s32[]{:T(128)}, f32[16,16]{0,1:T(8,128)S(1)}, f32[16,16]{1,0:T(8,128)S(1)}, s32[]{:T(128)}, s32[]{:T(128)}, /*index=5*/s32[]{:T(128)}) %tuple.1407), condition=%wide.region_47.48_spmd.clone.clone, body=%wide.region_46.47_spmd.clone.clone.sunk | while | flops 1476 | bytes 7039 | solution.py:26
  836.6 23.6 %while.620 = (s32[]{:T(128)}, f32[16,16]{0,1:T(8,128)S(1)}, f32[16,16]{1,0:T(8,128)S(1)}, s32[]{:T(128)}, s32[]{:T(128)}, /*index=5*/s32[]{:T(128)}) while((s32[]{:T(128)}, f32[16,16]{0,1:T(8,128)S(1)}, f32[16,16]{1,0:T(8,128)S(1)}, s32[]{:T(128)}, s32[]{:T(128)}, /*index=5*/s32[]{:T(128)}) %tuple.1413), condition=%wide.region_51.52_spmd.clone.clone, body=%wide.region_50.51_spmd.clone.clone.sunk | while | flops 1476 | bytes 7039 | solution.py:26
  860.2 23.2 %while.604 = (s32[]{:T(128)}, f32[16,16]{1,0:T(8,128)S(1)}, f32[16,16]{1,0:T(8,128)S(1)}, s32[]{:T(128)}, s32[]{:T(128)}, /*index=5*/s32[]{:T(128)}) while((s32[]{:T(128)}, f32[16,16]{1,0:T(8,128)S(1)}, f32[16,16]{1,0:T(8,128)S(1)}, s32[]{:T(128)}, s32[]{:T(128)}, /*index=5*/s32[]{:T(128)}) %tuple.1416), condition=%wide.region_53.54_spmd.clone, body=%wide.region_52.53_spmd.clone.sunk | while | flops 4196 | bytes 12656 | solution.py:41
  884.5 23.6 %while.621 = (s32[]{:T(128)}, f32[16,16]{0,1:T(8,128)S(1)}, f32[16,16]{1,0:T(8,128)S(1)}, s32[]{:T(128)}, s32[]{:T(128)}, /*index=5*/s32[]{:T(128)}) while((s32[]{:T(128)}, f32[16,16]{0,1:T(8,128)S(1)}, f32[16,16]{1,0:T(8,128)S(1)}, s32[]{:T(128)}, s32[]{:T(128)}, /*index=5*/s32[]{:T(128)}) %tuple.1419), condition=%wide.region_55.56_spmd.clone.clone, body=%wide.region_54.55_spmd.clone.clone.sunk | while | flops 1476 | bytes 7039 | solution.py:26
  908.2 23.2 %while.605 = (s32[]{:T(128)}, f32[16,16]{1,0:T(8,128)S(1)}, f32[16,16]{1,0:T(8,128)S(1)}, s32[]{:T(128)}, s32[]{:T(128)}, /*index=5*/s32[]{:T(128)}) while((s32[]{:T(128)}, f32[16,16]{1,0:T(8,128)S(1)}, f32[16,16]{1,0:T(8,128)S(1)}, s32[]{:T(128)}, s32[]{:T(128)}, /*index=5*/s32[]{:T(128)}) %tuple.1422), condition=%wide.region_57.58_spmd.clone, body=%wide.region_56.57_spmd.clone.sunk | while | flops 4196 | bytes 12656 | solution.py:41
  932.2 23.6 %while.622 = (s32[]{:T(128)}, f32[16,16]{0,1:T(8,128)S(1)}, f32[16,16]{1,0:T(8,128)S(1)}, s32[]{:T(128)}, s32[]{:T(128)}, /*index=5*/s32[]{:T(128)}) while((s32[]{:T(128)}, f32[16,16]{0,1:T(8,128)S(1)}, f32[16,16]{1,0:T(8,128)S(1)}, s32[]{:T(128)}, s32[]{:T(128)}, /*index=5*/s32[]{:T(128)}) %tuple.1425), condition=%wide.region_59.60_spmd.clone.clone, body=%wide.region_58.59_spmd.clone.clone.sunk | while | flops 1476 | bytes 7039 | solution.py:26
  979.7 23.6 %while.623 = (s32[]{:T(128)}, f32[16,16]{0,1:T(8,128)S(1)}, f32[16,16]{1,0:T(8,128)S(1)}, s32[]{:T(128)}, s32[]{:T(128)}, /*index=5*/s32[]{:T(128)}) while((s32[]{:T(128)}, f32[16,16]{0,1:T(8,128)S(1)}, f32[16,16]{1,0:T(8,128)S(1)}, s32[]{:T(128)}, s32[]{:T(128)}, /*index=5*/s32[]{:T(128)}) %tuple.1431), condition=%wide.region_63.64_spmd.clone.clone, body=%wide.region_62.63_spmd.clone.clone.sunk | while | flops 1476 | bytes 7039 | solution.py:26
  (2988 shorter events, 841.7 us)
Async XLA Ops:
  7.2 2.5 copy-start
  7.2 71.0 %all-reduce.33.cloned.1.call-start = ((), (), s32[]{:S(2)}) async-start(), calls=%async_computation | async-start | bytes 917504 | tf_op jit(solution)/shard_map/psum | solution.py:88
  16.6 7.8 copy-start.3
  28.7 231.9 %all-reduce.35.cloned.1.call-start = ((), (), s32[]{:S(2)}) async-start(), calls=%async_computation.1 | async-start | bytes 524288 | tf_op jit(solution)/shard_map/psum | solution.py:91
  260.5 385.3 %copy-start.2 = (f32[256,256]{1,0:T(8,128)S(1)}, f32[256,256]{1,0:T(8,128)}, u32[]{:S(2)}) copy-start(f32[256,256]{1,0:T(8,128)} %all-reduce.35.cloned.1.call-done) | copy-start | bytes 786436
  622.0 406.5 %copy-start.1 = (f32[448,256]{1,0:T(8,128)S(1)}, f32[448,256]{1,0:T(8,128)}, u32[]{:S(2)}) copy-start(f32[448,256]{1,0:T(8,128)} %all-reduce.33.cloned.1.call-done) | copy-start | bytes 1376260
Sparse Core Ops, SparseCore 0:
  28.8 49.3 all-reduce.32
  82.6 177.9 all-reduce.34
where the time goes:
time: 1040 us
  local copies, waits for them, and re-layouts  312 us (30%)
  waiting for transfers between devices  228 us (22%)
  matrix products  221 us (21%)
  loops' own time  184 us (18%)
  other arithmetic  75.4 us (7%)
  between operations  14.7 us (1%)
    dot_general x317, matrix products, high_dot(): jnp.dot(left, right, precision=lax.Precision.HIGHEST, preferred_element_t...  216 us
    another operation x16, loops' own time, cholesky_small(): lax.fori_loop(0, order, column_step, (matrix, jnp.zeros_like(matrix)))[1]  184 us
    psum x1, waiting for transfers between devices, body(): lower, inverse = cholesky_pair(lax.psum(gram, 'dom'))  179 us
    dynamic_slice x256, local copies, waits for them, and re-layouts, row_step(): pivot = lax.dynamic_slice_in_dim(row_lower, index, 1, 0)[0]  151 us
    dynamic_slice x256, local copies, waits for them, and re-layouts, column_step(): pivot = jnp.sqrt(lax.dynamic_slice_in_dim(column, index, 1, 0)[0])  150 us
    psum x1, waiting for transfers between devices, body(): coeffs = lax.psum(project(weighted, pose_bin, panels), 'rows')  49.3 us
  transfers between devices with their start and end apart: 2, of which 2 were waited for; matrix products, arithmetic and copies ran while one was open for 0% of the time, Pallas kernels for 0%

commit v1 on v0

v1 whole, which is shorter than its diff:
```python
import functools

import jax
import jax.numpy as jnp
from jax import lax
from jax.experimental import pallas as pl
from jax.experimental.pallas import tpu as pltpu
from jax.sharding import Mesh, PartitionSpec as P

F32 = jnp.float32
BF16 = jnp.bfloat16
HIGHEST = lax.Precision.HIGHEST

PART = 448
PIECE = 112
PIX = 6400
CHUNK = 640
GROUPS = 16
PROBES = 256


def three_terms(value):
    high = value.astype(BF16)
    rest = value - high.astype(F32)
    middle = rest.astype(BF16)
    low = (rest - middle.astype(F32)).astype(BF16)
    return high, middle, low


def project_kernel(
    place_ref, images_ref, panels_ref, mean_ref, ctf_ref, pose_ref, group_ref,
    own_ref, next_ref, across_ref, before_ref, total, picks, whole,
):
    step = pl.program_id(0)

    @pl.when(step == 0)
    def _():
        rows = lax.broadcasted_iota(jnp.int32, (128, PART), 0)
        group = jnp.broadcast_to(group_ref[...], (128, PART))
        pose = jnp.broadcast_to(pose_ref[...], (128, PART))
        wanted = jnp.where(rows < 3 * GROUPS, lax.rem(rows, GROUPS), 1)
        found = jnp.where(rows < 3 * GROUPS, group, pose)
        picks[...] = jnp.where(wanted == found, 1.0, 0.0).astype(F32).T
        total[...] = jnp.zeros_like(total)

    second = picks[:, 3 * GROUPS : 3 * GROUPS + 1] > 0.5
    stack = jnp.concatenate(three_terms(ctf_ref[...]), axis=0)
    ctf = jnp.dot(picks[:, : 3 * GROUPS].astype(BF16), stack, preferred_element_type=F32)
    mean = jnp.where(second, mean_ref[1:2, :], mean_ref[0:1, :])
    weighted = (ctf * (images_ref[...].astype(F32) - ctf * mean)).astype(BF16)
    for which in range(2):
        total[which] += jnp.dot(weighted, panels_ref[which], preferred_element_type=F32)

    @pl.when(step == pl.num_programs(0) - 1)
    def _():
        whole[...] = jnp.where(second, total[1], total[0])
        place = place_ref[0]
        for shift, out in enumerate((own_ref, next_ref, across_ref, before_ref)):
            first = pl.multiple_of(lax.rem(place + shift, 4) * PIECE, 16)
            out[...] = whole[pl.ds(first, PIECE), :]


def project(place, images, panels, mean_panels, ctf_table, pose_bin, ctf_group):
    piece = jax.ShapeDtypeStruct((PIECE, PROBES), F32)
    whole_piece = pl.BlockSpec((PIECE, PROBES), lambda k: (0, 0))
    return pl.pallas_call(
        project_kernel,
        grid=(PIX // CHUNK,),
        out_shape=(piece,) * 4,
        in_specs=[
            pl.BlockSpec(memory_space=pltpu.SMEM),
            pl.BlockSpec((PART, CHUNK), lambda k: (0, k)),
            pl.BlockSpec((2, CHUNK, PROBES), lambda k: (0, k, 0)),
            pl.BlockSpec((2, CHUNK), lambda k: (0, k)),
            pl.BlockSpec((GROUPS, CHUNK), lambda k: (0, k)),
            pl.BlockSpec((1, PART), lambda k: (0, 0)),
            pl.BlockSpec((1, PART), lambda k: (0, 0)),
        ],
        out_specs=(whole_piece,) * 4,
        scratch_shapes=[
            pltpu.VMEM((2, PART, PROBES), F32),
            pltpu.VMEM((PART, 128), F32),
            pltpu.VMEM((PART, PROBES), F32),
        ],
        compiler_params=pltpu.CompilerParams(vmem_limit_bytes=60 * 1024 * 1024),
        name="project",
    )(place, images, panels, mean_panels, ctf_table, pose_bin.reshape(1, PART), ctf_group.reshape(1, PART))


def gram_kernel(own_ref, first_ref, second_ref, third_ref, coeffs_ref, gram_ref, *, particles):
    coeffs = (own_ref[...] + first_ref[...]) + (second_ref[...] + third_ref[...])
    coeffs_ref[...] = coeffs
    gram = lax.dot_general(
        coeffs, coeffs, (((0,), (0,)), ((), ())), precision=HIGHEST, preferred_element_type=F32
    )
    gram_ref[...] = gram / particles


def gram_of(pieces, particles):
    return pl.pallas_call(
        functools.partial(gram_kernel, particles=particles),
        out_shape=(
            jax.ShapeDtypeStruct((PIECE, PROBES), F32),
            jax.ShapeDtypeStruct((PROBES, PROBES), F32),
        ),
        name="gram",
    )(*pieces)


def factor_kernel(place_ref, gram_ref, c0_ref, c1_ref, c2_ref, c3_ref, scores_ref, factor_ref, work, inv):
    lane = lax.broadcasted_iota(jnp.int32, (256, 256), 1)
    row = lax.broadcasted_iota(jnp.int32, (256, 256), 0)
    work[...] = gram_ref[...]
    inv[...] = jnp.where(lane == row, 1.0, 0.0).astype(F32)
    sub = lax.broadcasted_iota(jnp.int32, (8, 128), 0)

    def spread(value):
        return jnp.broadcast_to(value, (8, 128))

    for block in range(8):
        start = 32 * block
        half = block // 4
        if half == 0:
            tiles = ((work, 0), (work, 128), (inv, 0))
        else:
            tiles = ((work, 128), (inv, 0), (inv, 128))
        rows = [
            [ref[start + 8 * g : start + 8 * g + 8, col : col + 128] for ref, col in tiles]
            for g in range(4)
        ]
        for g in range(4):
            at = start - 128 * half + 8 * g
            cols = [
                {h: spread(rows[h][0][:, at + k : at + k + 1]) for h in range(g, 4)} for k in range(8)
            ]
            pivots = jnp.ones((8, 128), F32)
            for k in range(8):
                heads = {j: spread(cols[j][g][k : k + 1, :]) for j in range(k, 8)}
                pivots = jnp.where(sub == k, heads[k], pivots)
                inverse = 1.0 / heads[k]
                ratio = {h: cols[k][h] * inverse for h in range(g, 4)}
                ratio[g] = jnp.where(sub > k, ratio[g], 0.0)
                for j in range(k + 1, 8):
                    for h in range(g, 4):
                        cols[j][h] = cols[j][h] - ratio[h] * heads[j]
                for t in range(3):
                    head = spread(rows[g][t][k : k + 1, :])
                    for h in range(g, 4):
                        rows[h][t] = rows[h][t] - ratio[h] * head
            scale = lax.rsqrt(pivots)
            rows[g] = [value * scale for value in rows[g]]
        done = [jnp.concatenate([rows[g][t] for g in range(4)], axis=0) for t in range(3)]
        for (ref, col), value in zip(tiles, done):
            ref[start : start + 32, col : col + 128] = value
        if block == 7:
            break
        terms = [three_terms(value) for value in done]

        def left(t):
            high, middle, low = terms[t]
            return jnp.concatenate([high, high, middle, high, middle, low], axis=0)

        def right(ts):
            high, middle, low = (jnp.concatenate([terms[t][i] for t in ts], axis=1) for i in range(3))
            return jnp.concatenate([high, middle, high, low, middle, high], axis=0)

        def product(t, ts):
            return lax.dot_general(
                left(t), right(ts), (((0,), (0,)), ((), ())), preferred_element_type=F32
            )

        inside = start - 128 * half + 32
        if inside < 128:
            change = product(0, (0, 1, 2))
            for t, (ref, col) in enumerate(tiles):
                ref[start + 32 : 128 * half + 128, col : col + 128] -= change[inside:, 128 * t : 128 * t + 128]
        if half == 0:
            change = product(1, (1, 2))
            for t, (ref, col) in enumerate(tiles[1:]):
                ref[128:256, col : col + 128] -= change[:, 128 * t : 128 * t + 128]

    factor_ref[...] = jnp.where(row <= lane, work[...], 0.0)
    inverse = inv[...]
    place = place_ref[0]
    for shift, coeffs in enumerate((c0_ref, c1_ref, c2_ref, c3_ref)):
        first = pl.multiple_of(lax.rem(place + shift, 4) * PIECE, 16)
        scores_ref[pl.ds(first, PIECE), :] = lax.dot_general(
            coeffs[...], inverse, (((1,), (1,)), ((), ())), precision=HIGHEST, preferred_element_type=F32
        )


def factor_and_scores(place, gram, pieces):
    vmem = pl.BlockSpec(memory_space=pltpu.VMEM)
    return pl.pallas_call(
        factor_kernel,
        out_shape=(
            jax.ShapeDtypeStruct((PART, PROBES), F32),
            jax.ShapeDtypeStruct((PROBES, PROBES), F32),
        ),
        in_specs=[pl.BlockSpec(memory_space=pltpu.SMEM)] + [vmem] * 5,
        out_specs=(vmem, vmem),
        scratch_shapes=[pltpu.VMEM((PROBES, PROBES), F32), pltpu.VMEM((PROBES, PROBES), F32)],
        compiler_params=pltpu.CompilerParams(vmem_limit_bytes=32 * 1024 * 1024),
        name="factor",
    )(place, gram, *pieces)


def shifted(value, shift):
    return lax.ppermute(value, "x", [(i, (i + shift) % 4) for i in range(4)])


def sum_everywhere(gram):
    cut = gram.reshape(16, 16, PROBES)
    part = lax.all_to_all(cut, ("y", "x"), 0, 0, tiled=True).sum(0)
    part = part + lax.ppermute(part, "core", [(0, 1), (1, 0)])
    copies = jnp.broadcast_to(part[None], (8, 16, PROBES))
    part = lax.all_to_all(copies, "z", 0, 0, tiled=True).sum(0)
    copies = jnp.broadcast_to(part[None], (16, 16, PROBES))
    return lax.all_to_all(copies, ("y", "x"), 0, 0, tiled=True).reshape(PROBES, PROBES)


def body(images, panels, mean_panels, ctf_table, pose_bin, ctf_group):
    place = lax.axis_index("x").astype(jnp.int32).reshape(1)
    particles = PART * 64
    own, following, across, before = project(
        place, images, panels, mean_panels, ctf_table, pose_bin, ctf_group
    )
    across = shifted(across, 2)
    following = shifted(following, 1)
    before = shifted(before, 3)
    coeffs, gram = gram_of((own, following, across, before), particles)
    pieces = (coeffs, shifted(coeffs, 3), shifted(coeffs, 2), shifted(coeffs, 1))
    gram = sum_everywhere(gram)
    return factor_and_scores(place, gram, pieces)


def solution(mesh):
    fine = Mesh(mesh.devices.reshape(8, 4, 2, 4), ("z", "y", "core", "x"))
    dom = ("z", "y", "core")
    placed = (
        P(dom, "x"),
        P(dom, "x", None),
        P(dom, "x"),
        P(None, "x"),
        P(dom),
        P(dom),
    )
    return jax.shard_map(
        body, mesh=fine, in_specs=placed, out_specs=(P(dom, None), P()), check_vma=False
    )
```

time: 1040 us -> 85.2 us (0.08)
  the two profiles are of different devices: /device:TPU:1 before, /device:TPU:8 now
where the time goes in v1:
time: 85.2 us; the launch traced here: 84.7 us
  blocking collectives  31.4 us (37%)
  Pallas kernels  23.9 us (28%)
  starting transfers between devices  16.7 us (20%)
  waiting for transfers between devices  9.59 us (11%)
  local copies, waits for them, and re-layouts  2.33 us (3%)
    all_to_all x1, blocking collectives, sum_everywhere(): part = lax.all_to_all(copies, 'z', 0, 0, tiled=True).sum(0)  17.7 us
    all_to_all x1, blocking collectives, sum_everywhere(): part = lax.all_to_all(cut, ('y', 'x'), 0, 0, tiled=True).sum(0)  13.8 us
    pallas_call x1, Pallas kernels, project(): pl.pallas_call(project_kernel, grid=(PIX // CHUNK,), out_shape=(piece,) *...  12.2 us
    ppermute x6, starting transfers between devices, shifted(): return lax.ppermute(value, 'x', [(i, (i + shift) % 4) for i in range(4)])  11.3 us
    pallas_call x1, Pallas kernels, factor_and_scores(): pl.pallas_call(factor_kernel, out_shape=(jax.ShapeDtypeStruct((PART, PROB...  9.52 us
    ppermute x6, waiting for transfers between devices, shifted(): return lax.ppermute(value, 'x', [(i, (i + shift) % 4) for i in range(4)])  8.41 us
    all_to_all x1, starting transfers between devices, sum_everywhere(): lax.all_to_all(copies, ('y', 'x'), 0, 0, tiled=True).reshape(PROBES, PROBES)  5.33 us
    pallas_call x1, Pallas kernels, gram_of(): pl.pallas_call(functools.partial(gram_kernel, particles=particles), out_s...  2.19 us
  transfers between devices with their start and end apart: 8, of which 5 were waited for; matrix products, arithmetic and copies ran while one was open for 0% of the time, Pallas kernels for 0%

profile of v1, /device:TPU:8, one launch (start us, length us, event | category | flops | bytes accessed | tf_op | source)
XLA Modules:
  0.0 84.7 jit_solution(14872491404298914208)
XLA Ops:
  0.6 12.2 %project.1 = (f32[112,256]{1,0:T(8,128)}, f32[112,256]{1,0:T(8,128)}, f32[112,256]{1,0:T(8,128)}, f32[112,256]{1,0:T(8,128)}) custom-call(s32[1]{0:T(128)} %bitcast.place_ref, bf16[448,6400]{1,0:T(8,128)(2,1)} %images_ref.1, bf16[2,6400,256]{2,1,0:T(8,128)(2,1)} %panels_ref.1, f32[2,6400]{1,0:T(2,128)} %mean_ref.1, f32[16,6400]{1,0:T(8,128)} %ctf_ref.1, ...), custom_call_target="tpu_custom_call" | custom-call | tf_op jit(solution)/shard_map/project/pallas_call | solution.py:66
  12.9 1.5 %collective-permute-start = (f32[112,256]{1,0:T(8,128)}, f32[112,256]{1,0:T(8,128)S(1)}, u32[]{:S(2)}, u32[]{:S(2)}) collective-permute-start(f32[112,256]{1,0:T(8,128)} %get-tuple-element.9), channel_id=1, source_target_pairs={{0,1},{1,2},{2,3},{3,0},{4,5},{5,6},{6,7},{7,4},{8,9},{9,10},{10,1... | collective-permute-start | bytes 344072 | tf_op jit(solution)/shard_map/ppermute | solution.py:209
  14.4 2.7 %collective-permute-start.1 = (f32[112,256]{1,0:T(8,128)}, f32[112,256]{1,0:T(8,128)S(1)}, u32[]{:S(2)}, u32[]{:S(2)}) collective-permute-start(f32[112,256]{1,0:T(8,128)} %get-tuple-element.10), channel_id=1, source_target_pairs={{0,2},{1,3},{2,0},{3,1},{4,6},{5,7},{6,4},{7,5},{8,10},{9,11},{10,... | collective-permute-start | bytes 344072 | tf_op jit(solution)/shard_map/ppermute | solution.py:209
  17.1 1.4 %collective-permute-start.2 = (f32[112,256]{1,0:T(8,128)}, f32[112,256]{1,0:T(8,128)S(1)}, u32[]{:S(2)}, u32[]{:S(2)}) collective-permute-start(f32[112,256]{1,0:T(8,128)} %get-tuple-element.11), channel_id=1, source_target_pairs={{0,3},{1,0},{2,1},{3,2},{4,7},{5,4},{6,5},{7,6},{8,11},{9,8},{10,9... | collective-permute-start | bytes 344072 | tf_op jit(solution)/shard_map/ppermute | solution.py:209
  18.5 0.8 collective-permute-done.first_ref
  19.4 3.2 %collective-permute-done.1.second_ref = f32[112,256]{1,0:T(8,128)S(1)} collective-permute-done((f32[112,256]{1,0:T(8,128)}, f32[112,256]{1,0:T(8,128)S(1)}, u32[]{:S(2)}, u32[]{:S(2)}) %collective-permute-start.1) | collective-permute-done | bytes 114720 | tf_op jit(solution)/shard_map/ppermute | solution.py:209
  22.6 0.0 collective-permute-done.2.third_ref
  22.6 0.6 copy-done.2
  23.3 0.0 copy-done.3
  23.3 2.2 %gram.1 = (f32[112,256]{1,0:T(8,128)}, f32[256,256]{1,0:T(8,128)}) custom-call(f32[112,256]{1,0:T(8,128)} %get-tuple-element.8.own_ref, f32[112,256]{1,0:T(8,128)} %copy-done.1, f32[112,256]{1,0:T(8,128)} %copy-done.2, f32[112,256]{1,0:T(8,128)} %copy-done.3), custom_call_target="tpu_custom_call" | custom-call | tf_op jit(solution)/shard_map/gram/pallas_call | solution.py:100
  25.5 13.8 %all_to_all.15 = f32[16,16,256]{2,1,0:T(8,128)S(1)} all-to-all(f32[16,16,256]{2,1,0:T(8,128)} %bitcast.6), channel_id=1, replica_groups=mesh['z'=8,'y'=4,'core'=2,'x'=4] {'y','x'}, dimensions={0} | all-to-all | bytes 524288 | tf_op jit(solution)/shard_map/all_to_all | solution.py:214
  39.3 0.1 collective-permute-start.3
  39.4 1.2 %collective-permute-done.3 = f32[16,256]{1,0:T(8,128)S(1)} collective-permute-done((f32[16,256]{1,0:T(8,128)S(1)}, f32[16,256]{1,0:T(8,128)S(1)}, u32[]{:S(2)}, u32[]{:S(2)}) %collective-permute-start.3) | collective-permute-done | bytes 16416 | tf_op jit(solution)/shard_map/ppermute | solution.py:215
  40.6 17.7 %all_to_all.16 = f32[8,16,256]{2,1,0:T(8,128)S(1)} all-to-all(f32[8,16,256]{2,1,0:T(8,128)S(1)} %broadcast_in_dim.4), channel_id=1, replica_groups=mesh['z'=8,'y'=4,'core'=2,'x'=4] {'z'}, dimensions={0} | all-to-all | bytes 262144 | tf_op jit(solution)/shard_map/all_to_all | solution.py:217
  58.3 0.7 broadcast_in_dim.5
  59.0 5.3 %all-to-all-start.2 = ((f32[16,16,256]{2,1,0:T(8,128)}), f32[16,16,256]{2,1,0:T(8,128)S(1)}, u32[]{:S(2)}, u32[]{:S(2)}) async-start(f32[16,16,256]{2,1,0:T(8,128)} %broadcast_in_dim.5), calls=%async_computation.2 | async-start | bytes 524288 | tf_op jit(solution)/shard_map/all_to_all | solution.py:219
  64.3 1.5 %collective-permute-start.6 = (f32[112,256]{1,0:T(8,128)}, f32[112,256]{1,0:T(8,128)S(1)}, u32[]{:S(2)}, u32[]{:S(2)}) collective-permute-start(f32[112,256]{1,0:T(8,128)} %get-tuple-element.13.c0_ref), channel_id=1, source_target_pairs={{0,1},{1,2},{2,3},{3,0},{4,5},{5,6},{6,7},{7,4},{8,9},{9,10},{10,1... | collective-permute-start | bytes 344072 | tf_op jit(solution)/shard_map/ppermute | solution.py:209
  65.8 2.7 %collective-permute-start.5 = (f32[112,256]{1,0:T(8,128)}, f32[112,256]{1,0:T(8,128)S(1)}, u32[]{:S(2)}, u32[]{:S(2)}) collective-permute-start(f32[112,256]{1,0:T(8,128)} %get-tuple-element.13.c0_ref), channel_id=1, source_target_pairs={{0,2},{1,3},{2,0},{3,1},{4,6},{5,7},{6,4},{7,5},{8,10},{9,11},{10,... | collective-permute-start | bytes 344072 | tf_op jit(solution)/shard_map/ppermute | solution.py:209
  68.5 1.5 %collective-permute-start.4 = (f32[112,256]{1,0:T(8,128)}, f32[112,256]{1,0:T(8,128)S(1)}, u32[]{:S(2)}, u32[]{:S(2)}) collective-permute-start(f32[112,256]{1,0:T(8,128)} %get-tuple-element.13.c0_ref), channel_id=1, source_target_pairs={{0,3},{1,0},{2,1},{3,2},{4,7},{5,4},{6,5},{7,6},{8,11},{9,8},{10,9... | collective-permute-start | bytes 344072 | tf_op jit(solution)/shard_map/ppermute | solution.py:209
  70.0 2.8 %collective-permute-done.6.c3_ref = f32[112,256]{1,0:T(8,128)S(1)} collective-permute-done((f32[112,256]{1,0:T(8,128)}, f32[112,256]{1,0:T(8,128)S(1)}, u32[]{:S(2)}, u32[]{:S(2)}) %collective-permute-start.6) | collective-permute-done | bytes 114720 | tf_op jit(solution)/shard_map/ppermute | solution.py:209
  72.7 1.6 %collective-permute-done.5.c2_ref = f32[112,256]{1,0:T(8,128)S(1)} collective-permute-done((f32[112,256]{1,0:T(8,128)}, f32[112,256]{1,0:T(8,128)S(1)}, u32[]{:S(2)}, u32[]{:S(2)}) %collective-permute-start.5) | collective-permute-done | bytes 114720 | tf_op jit(solution)/shard_map/ppermute | solution.py:209
  74.3 0.0 all-to-all-done.2
  74.3 0.9 %copy-done = f32[112,256]{1,0:T(8,128)S(1)} copy-done((f32[112,256]{1,0:T(8,128)S(1)}, f32[112,256]{1,0:T(8,128)}, u32[]{:S(2)}) %copy-start) | copy-done | bytes 114712
  75.2 9.5 %factor.1 = (f32[448,256]{1,0:T(8,128)}, f32[256,256]{1,0:T(8,128)}) custom-call(s32[1]{0:T(128)} %bitcast.place_ref, f32[256,256]{1,0:T(8,128)S(1)} %bitcast.5, f32[112,256]{1,0:T(8,128)S(1)} %copy-done, f32[112,256]{1,0:T(8,128)S(1)} %collective-permute-done.4.c1_ref, f32[112,256]{1,0:T(8,128)S(1)} %collective-permute-done.5.c2_ref, ...), custom_call_target="tpu_custom_call" | custom-call | tf_op jit(solution)/shard_map/factor/pallas_call | solution.py:194
  (10 shorter events, 0.1 us)
Async XLA Ops:
  12.9 6.5 %collective-permute-start = (f32[112,256]{1,0:T(8,128)}, f32[112,256]{1,0:T(8,128)S(1)}, u32[]{:S(2)}, u32[]{:S(2)}) collective-permute-start(f32[112,256]{1,0:T(8,128)} %get-tuple-element.9), channel_id=1, source_target_pairs={{0,1},{1,2},{2,3},{3,0},{4,5},{5,6},{6,7},{7,4},{8,9},{9,10},{10,1... | collective-permute-start | bytes 344072 | tf_op jit(solution)/shard_map/ppermute | solution.py:209
  14.4 8.3 %collective-permute-start.1 = (f32[112,256]{1,0:T(8,128)}, f32[112,256]{1,0:T(8,128)S(1)}, u32[]{:S(2)}, u32[]{:S(2)}) collective-permute-start(f32[112,256]{1,0:T(8,128)} %get-tuple-element.10), channel_id=1, source_target_pairs={{0,2},{1,3},{2,0},{3,1},{4,6},{5,7},{6,4},{7,5},{8,10},{9,11},{10,... | collective-permute-start | bytes 344072 | tf_op jit(solution)/shard_map/ppermute | solution.py:209
  17.1 5.5 %collective-permute-start.2 = (f32[112,256]{1,0:T(8,128)}, f32[112,256]{1,0:T(8,128)S(1)}, u32[]{:S(2)}, u32[]{:S(2)}) collective-permute-start(f32[112,256]{1,0:T(8,128)} %get-tuple-element.11), channel_id=1, source_target_pairs={{0,3},{1,0},{2,1},{3,2},{4,7},{5,4},{6,5},{7,6},{8,11},{9,8},{10,9... | collective-permute-start | bytes 344072 | tf_op jit(solution)/shard_map/ppermute | solution.py:209
  19.4 3.3 %copy-start.1 = (f32[112,256]{1,0:T(8,128)}, f32[112,256]{1,0:T(8,128)S(1)}, u32[]{:S(2)}) copy-start(f32[112,256]{1,0:T(8,128)S(1)} %collective-permute-done.first_ref) | copy-start | bytes 344068
  22.6 0.7 copy-start.2
  22.6 0.7 copy-start.3
  39.3 1.3 %collective-permute-start.3 = (f32[16,256]{1,0:T(8,128)S(1)}, f32[16,256]{1,0:T(8,128)S(1)}, u32[]{:S(2)}, u32[]{:S(2)}) collective-permute-start(f32[16,256]{1,0:T(8,128)S(1)} %reduce_sum.18), channel_id=1, source_target_pairs={{0,4},{4,0},{1,5},{5,1},{2,6},{6,2},{3,7},{7,3},{8,12},{12,8},{9,1... | collective-permute-start | bytes 49160 | tf_op jit(solution)/shard_map/ppermute | solution.py:215
  59.0 15.3 %all-to-all-start.2 = ((f32[16,16,256]{2,1,0:T(8,128)}), f32[16,16,256]{2,1,0:T(8,128)S(1)}, u32[]{:S(2)}, u32[]{:S(2)}) async-start(f32[16,16,256]{2,1,0:T(8,128)} %broadcast_in_dim.5), calls=%async_computation.2 | async-start | bytes 524288 | tf_op jit(solution)/shard_map/all_to_all | solution.py:219
  64.3 8.4 %collective-permute-start.6 = (f32[112,256]{1,0:T(8,128)}, f32[112,256]{1,0:T(8,128)S(1)}, u32[]{:S(2)}, u32[]{:S(2)}) collective-permute-start(f32[112,256]{1,0:T(8,128)} %get-tuple-element.13.c0_ref), channel_id=1, source_target_pairs={{0,1},{1,2},{2,3},{3,0},{4,5},{5,6},{6,7},{7,4},{8,9},{9,10},{10,1... | collective-permute-start | bytes 344072 | tf_op jit(solution)/shard_map/ppermute | solution.py:209
  65.8 8.5 %collective-permute-start.5 = (f32[112,256]{1,0:T(8,128)}, f32[112,256]{1,0:T(8,128)S(1)}, u32[]{:S(2)}, u32[]{:S(2)}) collective-permute-start(f32[112,256]{1,0:T(8,128)} %get-tuple-element.13.c0_ref), channel_id=1, source_target_pairs={{0,2},{1,3},{2,0},{3,1},{4,6},{5,7},{6,4},{7,5},{8,10},{9,11},{10,... | collective-permute-start | bytes 344072 | tf_op jit(solution)/shard_map/ppermute | solution.py:209
  68.5 5.8 %collective-permute-start.4 = (f32[112,256]{1,0:T(8,128)}, f32[112,256]{1,0:T(8,128)S(1)}, u32[]{:S(2)}, u32[]{:S(2)}) collective-permute-start(f32[112,256]{1,0:T(8,128)} %get-tuple-element.13.c0_ref), channel_id=1, source_target_pairs={{0,3},{1,0},{2,1},{3,2},{4,7},{5,4},{6,5},{7,6},{8,11},{9,8},{10,9... | collective-permute-start | bytes 344072 | tf_op jit(solution)/shard_map/ppermute | solution.py:209
  74.3 0.9 %copy-start = (f32[112,256]{1,0:T(8,128)S(1)}, f32[112,256]{1,0:T(8,128)}, u32[]{:S(2)}) copy-start(f32[112,256]{1,0:T(8,128)} %get-tuple-element.13.c0_ref) | copy-start | bytes 344068

commit v2 on v1

v2 whole, which is shorter than its diff:
```python
import functools

import jax
import jax.numpy as jnp
from jax import lax
from jax.experimental import pallas as pl
from jax.experimental.pallas import tpu as pltpu
from jax.sharding import Mesh, PartitionSpec as P

F32 = jnp.float32
BF16 = jnp.bfloat16
HIGHEST = lax.Precision.HIGHEST

PART = 448
PIECE = 112
PIX = 6400
CUTS = (0, 2048, 4352, 6400)
STEP = 1280
GROUPS = 16
PROBES = 256
HALF = 192


def three_terms(value):
    high = value.astype(BF16)
    rest = value - high.astype(F32)
    middle = rest.astype(BF16)
    low = (rest - middle.astype(F32)).astype(BF16)
    return high, middle, low


def project_kernel(
    place_ref, pose_ref, group_ref, images_ref, panels_ref, mean_ref, ctf_ref,
    own_ref, next_ref, across_ref, before_ref,
    images, panels, mean, ctf, weighted, total, picks, whole, sems,
):
    chunks = [slice(first, last) for first, last in zip(CUTS[:-1], CUTS[1:])]
    copies = []
    for i, cut in enumerate(chunks):
        pairs = (
            (ctf_ref.at[:, cut], ctf.at[:, cut]),
            (mean_ref.at[:, cut], mean.at[:, cut]),
            (images_ref.at[:, cut], images.at[:, cut]),
            (panels_ref.at[0, cut, :], panels.at[0, cut, :]),
            (panels_ref.at[1, cut, :], panels.at[1, cut, :]),
        )
        copies.append([pltpu.make_async_copy(*pair, sems.at[i, j]) for j, pair in enumerate(pairs)])
    for copy in copies[0]:
        copy.start()

    rows = lax.broadcasted_iota(jnp.int32, (128, PART), 0)
    group = jnp.broadcast_to(group_ref[...], (128, PART))
    pose = jnp.broadcast_to(pose_ref[...], (128, PART))
    wanted = jnp.where(rows < 3 * GROUPS, lax.rem(rows, GROUPS), 1)
    found = jnp.where(rows < 3 * GROUPS, group, pose)
    picks[...] = jnp.where(wanted == found, 1.0, 0.0).astype(F32).T
    second = picks[:, 3 * GROUPS : 3 * GROUPS + 1] > 0.5
    chosen = picks[:, : 3 * GROUPS].astype(BF16)

    def weigh(cut):
        stack = jnp.concatenate(three_terms(ctf[:, cut]), axis=0)
        factor = jnp.dot(chosen, stack, preferred_element_type=F32)
        middle = jnp.where(second, mean[1:2, cut], mean[0:1, cut])
        weighted[:, cut] = (factor * (images[:, cut].astype(F32) - factor * middle)).astype(BF16)

    def add(cut):
        for which in range(2):
            part = jnp.dot(weighted[:, cut], panels[which, cut, :], preferred_element_type=F32)
            total[which] = part if cut.start == 0 else total[which] + part

    for i, chunk in enumerate(chunks):
        for copy in copies[i]:
            copy.wait()
        if i + 1 < len(chunks):
            for copy in copies[i + 1]:
                copy.start()
        cuts = [slice(at, min(at + STEP, chunk.stop)) for at in range(chunk.start, chunk.stop, STEP)]
        weigh(cuts[0])
        for j, cut in enumerate(cuts):
            if j + 1 < len(cuts):
                weigh(cuts[j + 1])
            add(cut)
    whole[...] = jnp.where(second, total[1], total[0])
    place = place_ref[0]
    for shift, out in enumerate((own_ref, next_ref, across_ref, before_ref)):
        first = pl.multiple_of(lax.rem(place + shift, 4) * PIECE, 16)
        out[...] = whole[pl.ds(first, PIECE), :]


def project(place, images, panels, mean_panels, ctf_table, pose_bin, ctf_group):
    piece = jax.ShapeDtypeStruct((PIECE, PROBES), F32)
    vmem = pl.BlockSpec(memory_space=pltpu.VMEM)
    anywhere = pl.BlockSpec(memory_space=pl.ANY)
    return pl.pallas_call(
        project_kernel,
        out_shape=(piece,) * 4,
        in_specs=[pl.BlockSpec(memory_space=pltpu.SMEM), vmem, vmem] + [anywhere] * 4,
        out_specs=(vmem,) * 4,
        scratch_shapes=[
            pltpu.VMEM((PART, PIX), BF16),
            pltpu.VMEM((2, PIX, PROBES), BF16),
            pltpu.VMEM((2, PIX), F32),
            pltpu.VMEM((GROUPS, PIX), F32),
            pltpu.VMEM((PART, PIX), BF16),
            pltpu.VMEM((2, PART, PROBES), F32),
            pltpu.VMEM((PART, 128), F32),
            pltpu.VMEM((PART, PROBES), F32),
            pltpu.SemaphoreType.DMA((len(CUTS) - 1, 5)),
        ],
        compiler_params=pltpu.CompilerParams(vmem_limit_bytes=60 * 1024 * 1024),
        name="project",
    )(place, pose_bin.reshape(1, PART), ctf_group.reshape(1, PART), images, panels, mean_panels, ctf_table)


def gram_kernel(core_ref, own_ref, first_ref, second_ref, third_ref, coeffs_ref, mine_ref, other_ref, packed, *, particles):
    coeffs = (own_ref[...] + first_ref[...]) + (second_ref[...] + third_ref[...])
    coeffs_ref[...] = coeffs

    def block(left, right):
        gram = lax.dot_general(
            left, right, (((0,), (0,)), ((), ())), precision=HIGHEST, preferred_element_type=F32
        )
        return gram / particles

    top = block(coeffs[:, :128], coeffs)
    packed[:128, :] = top[:, :128]
    packed[128:256, :] = top[:, 128:]
    packed[256:, :] = block(coeffs[:, 128:], coeffs[:, 128:])
    core = core_ref[0]
    mine_ref[...] = packed[pl.ds(pl.multiple_of(core * HALF, 8), HALF), :]
    other_ref[...] = packed[pl.ds(pl.multiple_of((1 - core) * HALF, 8), HALF), :]


def gram_of(core, pieces, particles):
    vmem = pl.BlockSpec(memory_space=pltpu.VMEM)
    return pl.pallas_call(
        functools.partial(gram_kernel, particles=particles),
        out_shape=(
            jax.ShapeDtypeStruct((PIECE, PROBES), F32),
            jax.ShapeDtypeStruct((HALF, 128), F32),
            jax.ShapeDtypeStruct((HALF, 128), F32),
        ),
        in_specs=[pl.BlockSpec(memory_space=pltpu.SMEM)] + [vmem] * 4,
        out_specs=(vmem,) * 3,
        scratch_shapes=[pltpu.VMEM((2 * HALF, 128), F32)],
        compiler_params=pltpu.CompilerParams(vmem_limit_bytes=12 * 1024 * 1024),
        name="gram",
    )(core, *pieces)


def factor_kernel(
    place_ref, core_ref, mine_ref, other_ref, c0_ref, c1_ref, c2_ref, c3_ref, scores_ref, factor_ref, work, inv
):
    lane = lax.broadcasted_iota(jnp.int32, (256, 256), 1)
    row = lax.broadcasted_iota(jnp.int32, (256, 256), 0)
    core = core_ref[0]
    work[pl.ds(pl.multiple_of(core * HALF, 8), HALF), :] = mine_ref[...]
    work[pl.ds(pl.multiple_of((1 - core) * HALF, 8), HALF), :] = other_ref[...]
    inv[...] = jnp.where(lane == row, 1.0, 0.0).astype(F32)
    sub = lax.broadcasted_iota(jnp.int32, (8, 128), 0)

    def spread(value):
        return jnp.broadcast_to(value, (8, 128))

    for block in range(8):
        start = 32 * block
        half = block // 4
        if half == 0:
            tiles = ((work, 0, 0), (work, 128, 0), (inv, 0, 0))
        else:
            tiles = ((work, 128, 0), (inv, 0, 0), (inv, 0, 128))
        rows = [
            [ref[start + low + 8 * g : start + low + 8 * g + 8, col : col + 128] for ref, low, col in tiles]
            for g in range(4)
        ]
        for g in range(4):
            at = start - 128 * half + 8 * g
            cols = [
                {h: spread(rows[h][0][:, at + k : at + k + 1]) for h in range(g, 4)} for k in range(8)
            ]
            pivots = jnp.ones((8, 128), F32)
            for k in range(8):
                heads = {j: spread(cols[j][g][k : k + 1, :]) for j in range(k, 8)}
                pivots = jnp.where(sub == k, heads[k], pivots)
                inverse = 1.0 / heads[k]
                ratio = {h: cols[k][h] * inverse for h in range(g, 4)}
                ratio[g] = jnp.where(sub > k, ratio[g], 0.0)
                for j in range(k + 1, 8):
                    for h in range(g, 4):
                        cols[j][h] = cols[j][h] - ratio[h] * heads[j]
                for t in range(3):
                    head = spread(rows[g][t][k : k + 1, :])
                    for h in range(g, 4):
                        rows[h][t] = rows[h][t] - ratio[h] * head
            scale = lax.rsqrt(pivots)
            rows[g] = [value * scale for value in rows[g]]
        done = [jnp.concatenate([rows[g][t] for g in range(4)], axis=0) for t in range(3)]
        for (ref, low, col), value in zip(tiles, done):
            ref[start + low : start + low + 32, col : col + 128] = value
        if block == 7:
            break
        terms = [three_terms(value) for value in done]

        def left(t):
            high, middle, low = terms[t]
            return jnp.concatenate([high, high, middle, high, middle, low], axis=0)

        def right(ts):
            high, middle, low = (jnp.concatenate([terms[t][i] for t in ts], axis=1) for i in range(3))
            return jnp.concatenate([high, middle, high, low, middle, high], axis=0)

        def product(t, ts):
            return lax.dot_general(
                left(t), right(ts), (((0,), (0,)), ((), ())), preferred_element_type=F32
            )

        inside = start - 128 * half + 32
        if inside < 128:
            change = product(0, (0, 1, 2))
            for t, (ref, low, col) in enumerate(tiles):
                last = 128 * half + 128 + low
                ref[start + 32 + low : last, col : col + 128] -= change[inside:, 128 * t : 128 * t + 128]
        if half == 0:
            change = product(1, (1, 2))
            for t, (ref, low, col) in enumerate(tiles[1:]):
                ref[128 + low : 256 + low, col : col + 128] -= change[:, 128 * t : 128 * t + 128]

    upper = row[:128, :128] <= lane[:128, :128]
    factor_ref[:128, :128] = jnp.where(upper, work[:128, :], 0.0)
    factor_ref[:128, 128:] = work[128:256, :]
    factor_ref[128:, :128] = jnp.zeros((128, 128), F32)
    factor_ref[128:, 128:] = jnp.where(upper, work[256:, :], 0.0)
    inverse = inv[...]
    place = place_ref[0]
    for shift, coeffs in enumerate((c0_ref, c1_ref, c2_ref, c3_ref)):
        first = pl.multiple_of(lax.rem(place + shift, 4) * PIECE, 16)
        scores_ref[pl.ds(first, PIECE), :] = lax.dot_general(
            coeffs[...], inverse, (((1,), (1,)), ((), ())), precision=HIGHEST, preferred_element_type=F32
        )


def factor_and_scores(place, core, halves, pieces):
    vmem = pl.BlockSpec(memory_space=pltpu.VMEM)
    return pl.pallas_call(
        factor_kernel,
        out_shape=(
            jax.ShapeDtypeStruct((PART, PROBES), F32),
            jax.ShapeDtypeStruct((PROBES, PROBES), F32),
        ),
        in_specs=[pl.BlockSpec(memory_space=pltpu.SMEM)] * 2 + [vmem] * 6,
        out_specs=(vmem, vmem),
        scratch_shapes=[pltpu.VMEM((2 * HALF, 128), F32), pltpu.VMEM((PROBES, PROBES), F32)],
        compiler_params=pltpu.CompilerParams(vmem_limit_bytes=12 * 1024 * 1024),
        name="factor",
    )(place, core, *halves, *pieces)


def shifted(value, shift):
    return lax.ppermute(value, "x", [(i, (i + shift) % 4) for i in range(4)])


def partner_of(step, z, y, core, x):
    if step < 4:
        flip = (1, 3)[step % 2]
        return (z, y, core, x ^ flip) if (step < 2) == (core == 0) else (z, y ^ flip, core, x)
    return (z ^ (1, 2, 6)[step - 4], y, core, x)


def exchanged(value, step):
    moves = []
    for z in range(8):
        for y in range(4):
            for core in range(2):
                for x in range(4):
                    to_z, to_y, to_core, to_x = partner_of(step, z, y, core, x)
                    source = ((z * 4 + y) * 2 + core) * 4 + x
                    moves.append((source, ((to_z * 4 + to_y) * 2 + to_core) * 4 + to_x))
    return lax.ppermute(value, ("z", "y", "core", "x"), moves)


def other_core(value):
    return lax.ppermute(value, "core", [(0, 1), (1, 0)])


def sum_everywhere(mine, other, coeffs):
    part = mine + other_core(other)
    for step in range(4):
        part = part + exchanged(part, step)
    pieces = []
    for step in range(4, 7):
        piece = shifted(coeffs, (2, 3, 1)[step - 4])
        part, piece = lax.optimization_barrier((part + exchanged(part, step), piece))
        pieces.append(piece)
    across, following, before = pieces
    return (part, other_core(part)), (following, across, before)


def body(images, panels, mean_panels, ctf_table, pose_bin, ctf_group):
    place = lax.axis_index("x").astype(jnp.int32).reshape(1)
    core = lax.axis_index("core").astype(jnp.int32).reshape(1)
    particles = PART * 64
    own, following, across, before = project(
        place, images, panels, mean_panels, ctf_table, pose_bin, ctf_group
    )
    across = shifted(across, 2)
    following = shifted(following, 1)
    before = shifted(before, 3)
    coeffs, mine, other = gram_of(core, (own, following, across, before), particles)
    halves, pieces = sum_everywhere(mine, other, coeffs)
    return factor_and_scores(place, core, halves, (coeffs, *pieces))


def solution(mesh):
    fine = Mesh(mesh.devices.reshape(8, 4, 2, 4), ("z", "y", "core", "x"))
    dom = ("z", "y", "core")
    placed = (
        P(dom, "x"),
        P(dom, "x", None),
        P(dom, "x"),
        P(None, "x"),
        P(dom),
        P(dom),
    )
    return jax.shard_map(
        body, mesh=fine, in_specs=placed, out_specs=(P(dom, None), P()), check_vma=False
    )
```

time: 85.2 us -> 78.8 us (0.925)
  the two profiles are of different devices: /device:TPU:8 before, /device:TPU:1 now
where the time goes in v2:
time: 78.8 us; the launch traced here: 78.6 us
  starting transfers between devices  35 us (44%)
  waiting for transfers between devices  21.5 us (27%)
  Pallas kernels  20.3 us (26%)
  local copies, waits for them, and re-layouts  0.9 us (1%)
    ppermute x7, waiting for transfers between devices, exchanged(): return lax.ppermute(value, ('z', 'y', 'core', 'x'), moves)  15.6 us
    ppermute x7, starting transfers between devices, exchanged(): return lax.ppermute(value, ('z', 'y', 'core', 'x'), moves)  15.3 us
    pallas_call x1, Pallas kernels, project(): pl.pallas_call(project_kernel, out_shape=(piece,) * 4, in_specs=[pl.Block...  10.4 us
    ppermute x2, starting transfers between devices, other_core(): return lax.ppermute(value, 'core', [(0, 1), (1, 0)])  10.1 us
    ppermute x6, starting transfers between devices, shifted(): return lax.ppermute(value, 'x', [(i, (i + shift) % 4) for i in range(4)])  9.61 us
    pallas_call x1, Pallas kernels, factor_and_scores(): pl.pallas_call(factor_kernel, out_shape=(jax.ShapeDtypeStruct((PART, PROB...  9.56 us
    ppermute x6, waiting for transfers between devices, shifted(): return lax.ppermute(value, 'x', [(i, (i + shift) % 4) for i in range(4)])  4.08 us
    ppermute x2, waiting for transfers between devices, other_core(): return lax.ppermute(value, 'core', [(0, 1), (1, 0)])  1.89 us
  transfers between devices with their start and end apart: 15, of which 10 were waited for; matrix products, arithmetic and copies ran while one was open for 0% of the time, Pallas kernels for 0%

profile of v2, /device:TPU:1, one launch (start us, length us, event | category | flops | bytes accessed | tf_op | source)
XLA Modules:
  0.0 78.6 jit_solution(10617735432553514630)
XLA Ops:
  0.6 10.4 %project.1 = (f32[112,256]{1,0:T(8,128)}, f32[112,256]{1,0:T(8,128)}, f32[112,256]{1,0:T(8,128)}, f32[112,256]{1,0:T(8,128)}) custom-call(s32[1]{0:T(128)} %bitcast.place_ref, s32[1,448]{1,0:T(1,128)} %bitcast.4, s32[1,448]{1,0:T(1,128)} %bitcast.5, bf16[448,6400]{1,0:T(8,128)(2,1)} %images_ref.1, bf16[2,6400,256]{2,1,0:T(8,128)(2,1)} %panels_ref.1, ...), custom_call_target="tpu_custom_call" | custom-call | tf_op jit(solution)/shard_map/project/pallas_call | solution.py:94
  11.0 2.1 %collective-permute-start = (f32[112,256]{1,0:T(8,128)}, f32[112,256]{1,0:T(8,128)S(1)}, u32[]{:S(2)}, u32[]{:S(2)}) collective-permute-start(f32[112,256]{1,0:T(8,128)} %get-tuple-element.16), channel_id=1, source_target_pairs={{0,1},{1,2},{2,3},{3,0},{4,5},{5,6},{6,7},{7,4},{8,9},{9,10},{10,1... | collective-permute-start | bytes 344072 | tf_op jit(solution)/shard_map/ppermute | solution.py:259
  13.2 2.5 %collective-permute-start.1 = (f32[112,256]{1,0:T(8,128)}, f32[112,256]{1,0:T(8,128)S(1)}, u32[]{:S(2)}, u32[]{:S(2)}) collective-permute-start(f32[112,256]{1,0:T(8,128)} %get-tuple-element.17), channel_id=1, source_target_pairs={{0,2},{1,3},{2,0},{3,1},{4,6},{5,7},{6,4},{7,5},{8,10},{9,11},{10,... | collective-permute-start | bytes 344072 | tf_op jit(solution)/shard_map/ppermute | solution.py:259
  15.6 1.1 %collective-permute-start.2 = (f32[112,256]{1,0:T(8,128)}, f32[112,256]{1,0:T(8,128)S(1)}, u32[]{:S(2)}, u32[]{:S(2)}) collective-permute-start(f32[112,256]{1,0:T(8,128)} %get-tuple-element.18), channel_id=1, source_target_pairs={{0,3},{1,0},{2,1},{3,2},{4,7},{5,4},{6,5},{7,6},{8,11},{9,8},{10,9... | collective-permute-start | bytes 344072 | tf_op jit(solution)/shard_map/ppermute | solution.py:259
  16.8 4.0 %collective-permute-done.1.second_ref = f32[112,256]{1,0:T(8,128)S(1)} collective-permute-done((f32[112,256]{1,0:T(8,128)}, f32[112,256]{1,0:T(8,128)S(1)}, u32[]{:S(2)}, u32[]{:S(2)}) %collective-permute-start.1) | collective-permute-done | bytes 114720 | tf_op jit(solution)/shard_map/ppermute | solution.py:259
  22.1 2.0 %collective-permute-start.3 = (f32[192,128]{1,0:T(8,128)S(1)}, f32[192,128]{1,0:T(8,128)S(1)}, u32[]{:S(2)}, u32[]{:S(2)}) collective-permute-start(f32[192,128]{1,0:T(8,128)S(1)} %get-tuple-element.20), channel_id=1, source_target_pairs={{0,4},{4,0},{1,5},{5,1},{2,6},{6,2},{3,7},{7,3},{8,12},{12,8},{9,1... | collective-permute-start | bytes 294920 | tf_op jit(solution)/shard_map/ppermute | solution.py:282
  24.1 0.9 %collective-permute-done.3 = f32[192,128]{1,0:T(8,128)S(1)} collective-permute-done((f32[192,128]{1,0:T(8,128)S(1)}, f32[192,128]{1,0:T(8,128)S(1)}, u32[]{:S(2)}, u32[]{:S(2)}) %collective-permute-start.3) | collective-permute-done | bytes 98336 | tf_op jit(solution)/shard_map/ppermute | solution.py:282
  25.1 1.0 %collective-permute-start.4 = (f32[192,128]{1,0:T(8,128)S(1)}, f32[192,128]{1,0:T(8,128)S(1)}, u32[]{:S(2)}, u32[]{:S(2)}) collective-permute-start(f32[192,128]{1,0:T(8,128)S(1)} %add.24), channel_id=1, source_target_pairs={{0,1},{1,0},{2,3},{3,2},{4,12},{5,13},{6,14},{7,15},{8,9},{9,8},{1... | collective-permute-start | bytes 294920 | tf_op jit(solution)/shard_map/ppermute | solution.py:278
  26.1 2.8 %collective-permute-done.4 = f32[192,128]{1,0:T(8,128)S(1)} collective-permute-done((f32[192,128]{1,0:T(8,128)S(1)}, f32[192,128]{1,0:T(8,128)S(1)}, u32[]{:S(2)}, u32[]{:S(2)}) %collective-permute-start.4) | collective-permute-done | bytes 98336 | tf_op jit(solution)/shard_map/ppermute | solution.py:278
  29.0 2.5 %collective-permute-start.5 = (f32[192,128]{1,0:T(8,128)S(1)}, f32[192,128]{1,0:T(8,128)S(1)}, u32[]{:S(2)}, u32[]{:S(2)}) collective-permute-start(f32[192,128]{1,0:T(8,128)S(1)} %add.25), channel_id=1, source_target_pairs={{0,3},{1,2},{2,1},{3,0},{4,28},{5,29},{6,30},{7,31},{8,11},{9,10},... | collective-permute-start | bytes 294920 | tf_op jit(solution)/shard_map/ppermute | solution.py:278
  31.4 2.3 %collective-permute-done.5 = f32[192,128]{1,0:T(8,128)S(1)} collective-permute-done((f32[192,128]{1,0:T(8,128)S(1)}, f32[192,128]{1,0:T(8,128)S(1)}, u32[]{:S(2)}, u32[]{:S(2)}) %collective-permute-start.5) | collective-permute-done | bytes 98336 | tf_op jit(solution)/shard_map/ppermute | solution.py:278
  33.7 1.1 %collective-permute-start.6 = (f32[192,128]{1,0:T(8,128)S(1)}, f32[192,128]{1,0:T(8,128)S(1)}, u32[]{:S(2)}, u32[]{:S(2)}) collective-permute-start(f32[192,128]{1,0:T(8,128)S(1)} %add.26), channel_id=1, source_target_pairs={{0,8},{1,9},{2,10},{3,11},{4,5},{5,4},{6,7},{7,6},{8,0},{9,1},{10,... | collective-permute-start | bytes 294920 | tf_op jit(solution)/shard_map/ppermute | solution.py:278
  34.8 2.5 %collective-permute-done.6 = f32[192,128]{1,0:T(8,128)S(1)} collective-permute-done((f32[192,128]{1,0:T(8,128)S(1)}, f32[192,128]{1,0:T(8,128)S(1)}, u32[]{:S(2)}, u32[]{:S(2)}) %collective-permute-start.6) | collective-permute-done | bytes 98336 | tf_op jit(solution)/shard_map/ppermute | solution.py:278
  37.3 2.4 %collective-permute-start.7 = (f32[192,128]{1,0:T(8,128)S(1)}, f32[192,128]{1,0:T(8,128)S(1)}, u32[]{:S(2)}, u32[]{:S(2)}) collective-permute-start(f32[192,128]{1,0:T(8,128)S(1)} %add.27), channel_id=1, source_target_pairs={{0,24},{1,25},{2,26},{3,27},{4,7},{5,6},{6,5},{7,4},{8,16},{9,17},... | collective-permute-start | bytes 294920 | tf_op jit(solution)/shard_map/ppermute | solution.py:278
  40.2 2.3 %collective-permute-done.7 = f32[192,128]{1,0:T(8,128)S(1)} collective-permute-done((f32[192,128]{1,0:T(8,128)S(1)}, f32[192,128]{1,0:T(8,128)S(1)}, u32[]{:S(2)}, u32[]{:S(2)}) %collective-permute-start.7) | collective-permute-done | bytes 98336 | tf_op jit(solution)/shard_map/ppermute | solution.py:278
  42.5 1.0 %collective-permute-start.8 = (f32[192,128]{1,0:T(8,128)S(1)}, f32[192,128]{1,0:T(8,128)S(1)}, u32[]{:S(2)}, u32[]{:S(2)}) collective-permute-start(f32[192,128]{1,0:T(8,128)S(1)} %add.28), channel_id=1, source_target_pairs={{0,32},{1,33},{2,34},{3,35},{4,36},{5,37},{6,38},{7,39},{8,40},{9,... | collective-permute-start | bytes 294920 | tf_op jit(solution)/shard_map/ppermute | solution.py:278
  43.5 3.4 %collective-permute-start.11 = (f32[112,256]{1,0:T(8,128)S(1)}, f32[112,256]{1,0:T(8,128)S(1)}, u32[]{:S(2)}, u32[]{:S(2)}) collective-permute-start(f32[112,256]{1,0:T(8,128)S(1)} %get-tuple-element.21.c0_ref), channel_id=1, source_target_pairs={{0,3},{1,0},{2,1},{3,2},{4,7},{5,4},{6,5},{7,6},{8,11},{9,8},{10,9... | collective-permute-start | bytes 344072 | tf_op jit(solution)/shard_map/ppermute | solution.py:259
  46.9 3.1 %collective-permute-start.10 = (f32[192,128]{1,0:T(8,128)S(1)}, f32[192,128]{1,0:T(8,128)S(1)}, u32[]{:S(2)}, u32[]{:S(2)}) collective-permute-start(f32[192,128]{1,0:T(8,128)S(1)} %add.29), channel_id=1, source_target_pairs={{0,64},{1,65},{2,66},{3,67},{4,68},{5,69},{6,70},{7,71},{8,72},{9,... | collective-permute-start | bytes 294920 | tf_op jit(solution)/shard_map/ppermute | solution.py:278
  50.0 3.1 %collective-permute-done.10 = f32[192,128]{1,0:T(8,128)S(1)} collective-permute-done((f32[192,128]{1,0:T(8,128)S(1)}, f32[192,128]{1,0:T(8,128)S(1)}, u32[]{:S(2)}, u32[]{:S(2)}) %collective-permute-start.10) | collective-permute-done | bytes 98336 | tf_op jit(solution)/shard_map/ppermute | solution.py:278
  53.1 4.3 %collective-permute-start.12 = (f32[192,128]{1,0:T(8,128)S(1)}, f32[192,128]{1,0:T(8,128)S(1)}, u32[]{:S(2)}, u32[]{:S(2)}) collective-permute-start(f32[192,128]{1,0:T(8,128)S(1)} %add.30), channel_id=1, source_target_pairs={{0,192},{1,193},{2,194},{3,195},{4,196},{5,197},{6,198},{7,199},{8... | collective-permute-start | bytes 294920 | tf_op jit(solution)/shard_map/ppermute | solution.py:278
  57.4 2.6 %collective-permute-done.12 = f32[192,128]{1,0:T(8,128)S(1)} collective-permute-done((f32[192,128]{1,0:T(8,128)S(1)}, f32[192,128]{1,0:T(8,128)S(1)}, u32[]{:S(2)}, u32[]{:S(2)}) %collective-permute-start.12) | collective-permute-done | bytes 98336 | tf_op jit(solution)/shard_map/ppermute | solution.py:278
  60.0 8.1 %collective-permute-start.14 = (f32[192,128]{1,0:T(8,128)S(1)}, f32[192,128]{1,0:T(8,128)S(1)}, u32[]{:S(2)}, u32[]{:S(2)}) collective-permute-start(f32[192,128]{1,0:T(8,128)S(1)} %add.31.mine_ref), channel_id=1, source_target_pairs={{0,4},{4,0},{1,5},{5,1},{2,6},{6,2},{3,7},{7,3},{8,12},{12,8},{9,1... | collective-permute-start | bytes 294920 | tf_op jit(solution)/shard_map/ppermute | solution.py:282
  68.1 0.9 %collective-permute-done.14.other_ref = f32[192,128]{1,0:T(8,128)S(1)} collective-permute-done((f32[192,128]{1,0:T(8,128)S(1)}, f32[192,128]{1,0:T(8,128)S(1)}, u32[]{:S(2)}, u32[]{:S(2)}) %collective-permute-start.14) | collective-permute-done | bytes 98336 | tf_op jit(solution)/shard_map/ppermute | solution.py:282
  69.1 9.6 %factor.1 = (f32[448,256]{1,0:T(8,128)}, f32[256,256]{1,0:T(8,128)}) custom-call(s32[1]{0:T(128)} %bitcast.place_ref, s32[1]{0:T(128)} %bitcast.1.core_ref, f32[192,128]{1,0:T(8,128)S(1)} %add.31.mine_ref, f32[192,128]{1,0:T(8,128)S(1)} %collective-permute-done.14.other_ref, f32[112,256]{1,0:T(8,128)S(1)} %get-tuple-element.21.c0_ref, ...), custom_call_target="tpu_custom_call" | custom-call | tf_op jit(solution)/shard_map/factor/pallas_call | solution.py:244
  (19 shorter events, 1.9 us)
Async XLA Ops:
  11.0 5.8 %collective-permute-start = (f32[112,256]{1,0:T(8,128)}, f32[112,256]{1,0:T(8,128)S(1)}, u32[]{:S(2)}, u32[]{:S(2)}) collective-permute-start(f32[112,256]{1,0:T(8,128)} %get-tuple-element.16), channel_id=1, source_target_pairs={{0,1},{1,2},{2,3},{3,0},{4,5},{5,6},{6,7},{7,4},{8,9},{9,10},{10,1... | collective-permute-start | bytes 344072 | tf_op jit(solution)/shard_map/ppermute | solution.py:259
  13.2 7.7 %collective-permute-start.1 = (f32[112,256]{1,0:T(8,128)}, f32[112,256]{1,0:T(8,128)S(1)}, u32[]{:S(2)}, u32[]{:S(2)}) collective-permute-start(f32[112,256]{1,0:T(8,128)} %get-tuple-element.17), channel_id=1, source_target_pairs={{0,2},{1,3},{2,0},{3,1},{4,6},{5,7},{6,4},{7,5},{8,10},{9,11},{10,... | collective-permute-start | bytes 344072 | tf_op jit(solution)/shard_map/ppermute | solution.py:259
  15.6 5.2 %collective-permute-start.2 = (f32[112,256]{1,0:T(8,128)}, f32[112,256]{1,0:T(8,128)S(1)}, u32[]{:S(2)}, u32[]{:S(2)}) collective-permute-start(f32[112,256]{1,0:T(8,128)} %get-tuple-element.18), channel_id=1, source_target_pairs={{0,3},{1,0},{2,1},{3,2},{4,7},{5,4},{6,5},{7,6},{8,11},{9,8},{10,9... | collective-permute-start | bytes 344072 | tf_op jit(solution)/shard_map/ppermute | solution.py:259
  20.8 0.9 %copy-start = (f32[112,256]{1,0:T(8,128)S(1)}, f32[112,256]{1,0:T(8,128)}, u32[]{:S(2)}) copy-start(f32[112,256]{1,0:T(8,128)} %get-tuple-element.15.own_ref) | copy-start | bytes 344068
  22.1 2.9 %collective-permute-start.3 = (f32[192,128]{1,0:T(8,128)S(1)}, f32[192,128]{1,0:T(8,128)S(1)}, u32[]{:S(2)}, u32[]{:S(2)}) collective-permute-start(f32[192,128]{1,0:T(8,128)S(1)} %get-tuple-element.20), channel_id=1, source_target_pairs={{0,4},{4,0},{1,5},{5,1},{2,6},{6,2},{3,7},{7,3},{8,12},{12,8},{9,1... | collective-permute-start | bytes 294920 | tf_op jit(solution)/shard_map/ppermute | solution.py:282
  25.1 3.8 %collective-permute-start.4 = (f32[192,128]{1,0:T(8,128)S(1)}, f32[192,128]{1,0:T(8,128)S(1)}, u32[]{:S(2)}, u32[]{:S(2)}) collective-permute-start(f32[192,128]{1,0:T(8,128)S(1)} %add.24), channel_id=1, source_target_pairs={{0,1},{1,0},{2,3},{3,2},{4,12},{5,13},{6,14},{7,15},{8,9},{9,8},{1... | collective-permute-start | bytes 294920 | tf_op jit(solution)/shard_map/ppermute | solution.py:278
  29.0 4.8 %collective-permute-start.5 = (f32[192,128]{1,0:T(8,128)S(1)}, f32[192,128]{1,0:T(8,128)S(1)}, u32[]{:S(2)}, u32[]{:S(2)}) collective-permute-start(f32[192,128]{1,0:T(8,128)S(1)} %add.25), channel_id=1, source_target_pairs={{0,3},{1,2},{2,1},{3,0},{4,28},{5,29},{6,30},{7,31},{8,11},{9,10},... | collective-permute-start | bytes 294920 | tf_op jit(solution)/shard_map/ppermute | solution.py:278
  33.7 3.6 %collective-permute-start.6 = (f32[192,128]{1,0:T(8,128)S(1)}, f32[192,128]{1,0:T(8,128)S(1)}, u32[]{:S(2)}, u32[]{:S(2)}) collective-permute-start(f32[192,128]{1,0:T(8,128)S(1)} %add.26), channel_id=1, source_target_pairs={{0,8},{1,9},{2,10},{3,11},{4,5},{5,4},{6,7},{7,6},{8,0},{9,1},{10,... | collective-permute-start | bytes 294920 | tf_op jit(solution)/shard_map/ppermute | solution.py:278
  37.3 5.2 %collective-permute-start.7 = (f32[192,128]{1,0:T(8,128)S(1)}, f32[192,128]{1,0:T(8,128)S(1)}, u32[]{:S(2)}, u32[]{:S(2)}) collective-permute-start(f32[192,128]{1,0:T(8,128)S(1)} %add.27), channel_id=1, source_target_pairs={{0,24},{1,25},{2,26},{3,27},{4,7},{5,6},{6,5},{7,4},{8,16},{9,17},... | collective-permute-start | bytes 294920 | tf_op jit(solution)/shard_map/ppermute | solution.py:278
  39.7 7.2 %collective-permute-start.9 = (f32[112,256]{1,0:T(8,128)S(1)}, f32[112,256]{1,0:T(8,128)S(1)}, u32[]{:S(2)}, u32[]{:S(2)}) collective-permute-start(f32[112,256]{1,0:T(8,128)S(1)} %get-tuple-element.21.c0_ref), channel_id=1, source_target_pairs={{0,2},{1,3},{2,0},{3,1},{4,6},{5,7},{6,4},{7,5},{8,10},{9,11},{10,... | collective-permute-start | bytes 344072 | tf_op jit(solution)/shard_map/ppermute | solution.py:259
  42.5 4.4 %collective-permute-start.8 = (f32[192,128]{1,0:T(8,128)S(1)}, f32[192,128]{1,0:T(8,128)S(1)}, u32[]{:S(2)}, u32[]{:S(2)}) collective-permute-start(f32[192,128]{1,0:T(8,128)S(1)} %add.28), channel_id=1, source_target_pairs={{0,32},{1,33},{2,34},{3,35},{4,36},{5,37},{6,38},{7,39},{8,40},{9,... | collective-permute-start | bytes 294920 | tf_op jit(solution)/shard_map/ppermute | solution.py:278
  43.5 9.6 %collective-permute-start.11 = (f32[112,256]{1,0:T(8,128)S(1)}, f32[112,256]{1,0:T(8,128)S(1)}, u32[]{:S(2)}, u32[]{:S(2)}) collective-permute-start(f32[112,256]{1,0:T(8,128)S(1)} %get-tuple-element.21.c0_ref), channel_id=1, source_target_pairs={{0,3},{1,0},{2,1},{3,2},{4,7},{5,4},{6,5},{7,6},{8,11},{9,8},{10,9... | collective-permute-start | bytes 344072 | tf_op jit(solution)/shard_map/ppermute | solution.py:259
  46.9 6.1 %collective-permute-start.10 = (f32[192,128]{1,0:T(8,128)S(1)}, f32[192,128]{1,0:T(8,128)S(1)}, u32[]{:S(2)}, u32[]{:S(2)}) collective-permute-start(f32[192,128]{1,0:T(8,128)S(1)} %add.29), channel_id=1, source_target_pairs={{0,64},{1,65},{2,66},{3,67},{4,68},{5,69},{6,70},{7,71},{8,72},{9,... | collective-permute-start | bytes 294920 | tf_op jit(solution)/shard_map/ppermute | solution.py:278
  50.0 10.0 %collective-permute-start.13 = (f32[112,256]{1,0:T(8,128)S(1)}, f32[112,256]{1,0:T(8,128)S(1)}, u32[]{:S(2)}, u32[]{:S(2)}) collective-permute-start(f32[112,256]{1,0:T(8,128)S(1)} %get-tuple-element.21.c0_ref), channel_id=1, source_target_pairs={{0,1},{1,2},{2,3},{3,0},{4,5},{5,6},{6,7},{7,4},{8,9},{9,10},{10,1... | collective-permute-start | bytes 344072 | tf_op jit(solution)/shard_map/ppermute | solution.py:259
  53.1 6.9 %collective-permute-start.12 = (f32[192,128]{1,0:T(8,128)S(1)}, f32[192,128]{1,0:T(8,128)S(1)}, u32[]{:S(2)}, u32[]{:S(2)}) collective-permute-start(f32[192,128]{1,0:T(8,128)S(1)} %add.30), channel_id=1, source_target_pairs={{0,192},{1,193},{2,194},{3,195},{4,196},{5,197},{6,198},{7,199},{8... | collective-permute-start | bytes 294920 | tf_op jit(solution)/shard_map/ppermute | solution.py:278
  60.0 9.0 %collective-permute-start.14 = (f32[192,128]{1,0:T(8,128)S(1)}, f32[192,128]{1,0:T(8,128)S(1)}, u32[]{:S(2)}, u32[]{:S(2)}) collective-permute-start(f32[192,128]{1,0:T(8,128)S(1)} %add.31.mine_ref), channel_id=1, source_target_pairs={{0,4},{4,0},{1,5},{5,1},{2,6},{6,2},{3,7},{7,3},{8,12},{12,8},{9,1... | collective-permute-start | bytes 294920 | tf_op jit(solution)/shard_map/ppermute | solution.py:282

commit v3 on v2

--- a/solution.py
+++ b/solution.py
@@ -30,9 +30,9 @@
 
 
 def project_kernel(
-    place_ref, pose_ref, group_ref, images_ref, panels_ref, mean_ref, ctf_ref,
+    pose_ref, group_ref, images_ref, panels_ref, mean_ref, ctf_ref,
     own_ref, next_ref, across_ref, before_ref,
-    images, panels, mean, ctf, weighted, total, picks, whole, sems,
+    pose_in, group_in, images, panels, mean, ctf, weighted, total, picks, whole, sems, index_sems,
 ):
     chunks = [slice(first, last) for first, last in zip(CUTS[:-1], CUTS[1:])]
     copies = []
@@ -45,12 +45,18 @@
             (panels_ref.at[1, cut, :], panels.at[1, cut, :]),
         )
         copies.append([pltpu.make_async_copy(*pair, sems.at[i, j]) for j, pair in enumerate(pairs)])
-    for copy in copies[0]:
+    indices = (
+        pltpu.make_async_copy(pose_ref, pose_in, index_sems.at[0]),
+        pltpu.make_async_copy(group_ref, group_in, index_sems.at[1]),
+    )
+    for copy in (*indices, *copies[0]):
         copy.start()
+    for copy in indices:
+        copy.wait()
 
     rows = lax.broadcasted_iota(jnp.int32, (128, PART), 0)
-    group = jnp.broadcast_to(group_ref[...], (128, PART))
-    pose = jnp.broadcast_to(pose_ref[...], (128, PART))
+    group = jnp.broadcast_to(group_in[...], (128, PART))
+    pose = jnp.broadcast_to(pose_in[...], (128, PART))
     wanted = jnp.where(rows < 3 * GROUPS, lax.rem(rows, GROUPS), 1)
     found = jnp.where(rows < 3 * GROUPS, group, pose)
     picks[...] = jnp.where(wanted == found, 1.0, 0.0).astype(F32).T
@@ -69,34 +75,38 @@
             total[which] = part if cut.start == 0 else total[which] + part
 
     for i, chunk in enumerate(chunks):
-        for copy in copies[i]:
+        for copy in copies[i][:3]:
             copy.wait()
         if i + 1 < len(chunks):
             for copy in copies[i + 1]:
                 copy.start()
         cuts = [slice(at, min(at + STEP, chunk.stop)) for at in range(chunk.start, chunk.stop, STEP)]
         weigh(cuts[0])
+        for copy in copies[i][3:]:
+            copy.wait()
         for j, cut in enumerate(cuts):
             if j + 1 < len(cuts):
                 weigh(cuts[j + 1])
             add(cut)
     whole[...] = jnp.where(second, total[1], total[0])
-    place = place_ref[0]
+    place = lax.axis_index("x")
     for shift, out in enumerate((own_ref, next_ref, across_ref, before_ref)):
         first = pl.multiple_of(lax.rem(place + shift, 4) * PIECE, 16)
         out[...] = whole[pl.ds(first, PIECE), :]
 
 
-def project(place, images, panels, mean_panels, ctf_table, pose_bin, ctf_group):
+def project(images, panels, mean_panels, ctf_table, pose_bin, ctf_group):
     piece = jax.ShapeDtypeStruct((PIECE, PROBES), F32)
     vmem = pl.BlockSpec(memory_space=pltpu.VMEM)
     anywhere = pl.BlockSpec(memory_space=pl.ANY)
     return pl.pallas_call(
         project_kernel,
         out_shape=(piece,) * 4,
-        in_specs=[pl.BlockSpec(memory_space=pltpu.SMEM), vmem, vmem] + [anywhere] * 4,
+        in_specs=[anywhere] * 6,
         out_specs=(vmem,) * 4,
         scratch_shapes=[
+            pltpu.VMEM((1, PART), jnp.int32),
+            pltpu.VMEM((1, PART), jnp.int32),
             pltpu.VMEM((PART, PIX), BF16),
             pltpu.VMEM((2, PIX, PROBES), BF16),
             pltpu.VMEM((2, PIX), F32),
@@ -106,10 +116,27 @@
             pltpu.VMEM((PART, 128), F32),
             pltpu.VMEM((PART, PROBES), F32),
             pltpu.SemaphoreType.DMA((len(CUTS) - 1, 5)),
+            pltpu.SemaphoreType.DMA((2,)),
         ],
         compiler_params=pltpu.CompilerParams(vmem_limit_bytes=60 * 1024 * 1024),
         name="project",
-    )(place, pose_bin.reshape(1, PART), ctf_group.reshape(1, PART), images, panels, mean_panels, ctf_table)
+    )(pose_bin.reshape(1, PART), ctf_group.reshape(1, PART), images, panels, mean_panels, ctf_table)
+
+
+def keep_kernel(piece_ref, kept_ref):
+    kept_ref[...] = piece_ref[...]
+
+
+def kept(piece):
+    vmem = pl.BlockSpec(memory_space=pltpu.VMEM)
+    return pl.pallas_call(
+        keep_kernel,
+        out_shape=jax.ShapeDtypeStruct(piece.shape, piece.dtype),
+        in_specs=[vmem],
+        out_specs=vmem,
+        compiler_params=pltpu.CompilerParams(vmem_limit_bytes=2 * 1024 * 1024),
+        name="keep",
+    )(piece)
 
 
 def gram_kernel(core_ref, own_ref, first_ref, second_ref, third_ref, coeffs_ref, mine_ref, other_ref, packed, *, particles):
@@ -230,12 +257,15 @@
     factor_ref[:128, 128:] = work[128:256, :]
     factor_ref[128:, :128] = jnp.zeros((128, 128), F32)
     factor_ref[128:, 128:] = jnp.where(upper, work[256:, :], 0.0)
-    inverse = inv[...]
+    high, middle, _ = three_terms(inv[...])
+    right = jnp.concatenate([high, middle, high], axis=1)
     place = place_ref[0]
     for shift, coeffs in enumerate((c0_ref, c1_ref, c2_ref, c3_ref)):
         first = pl.multiple_of(lax.rem(place + shift, 4) * PIECE, 16)
+        high, middle, _ = three_terms(coeffs[...])
+        left_side = jnp.concatenate([high, high, middle], axis=1)
         scores_ref[pl.ds(first, PIECE), :] = lax.dot_general(
-            coeffs[...], inverse, (((1,), (1,)), ((), ())), precision=HIGHEST, preferred_element_type=F32
+            left_side, right, (((1,), (1,)), ((), ())), preferred_element_type=F32
         )
 
 
@@ -300,12 +330,12 @@
     core = lax.axis_index("core").astype(jnp.int32).reshape(1)
     particles = PART * 64
     own, following, across, before = project(
-        place, images, panels, mean_panels, ctf_table, pose_bin, ctf_group
+        images, panels, mean_panels, ctf_table, pose_bin, ctf_group
     )
     across = shifted(across, 2)
     following = shifted(following, 1)
     before = shifted(before, 3)
-    coeffs, mine, other = gram_of(core, (own, following, across, before), particles)
+    coeffs, mine, other = gram_of(core, (kept(own), following, across, before), particles)
     halves, pieces = sum_everywhere(mine, other, coeffs)
     return factor_and_scores(place, core, halves, (coeffs, *pieces))
 

time: 78.8 us -> 75.8 us (0.962)
  Pallas kernels: 20.3 us -> 18.3 us
  waiting for transfers between devices: 21.5 us -> 20.6 us
    pallas_call x1 -> x2, Pallas kernels: 10.4 us -> 8.8 us  [the longest x1 8.79 us: project(): pl.pallas_call(project_kernel, out_shape=(piece,) * 4, in_specs=[anywhere...]
    ppermute x6, waiting for transfers between devices: 4.08 us -> 3.15 us  [shifted(): return lax.ppermute(value, 'x', [(i, (i + shift) % 4) for i in range(4)])]
  transfers between devices with their start and end apart: 15 -> 15, of which waited for: 10 -> 9; matrix products, arithmetic and copies ran while one was open for 0% -> 0% of each run, Pallas kernels for 0% -> 0%
where the time goes in v3:
time: 75.8 us; the launch traced here: 75.6 us
  starting transfers between devices  35.1 us (46%)
  waiting for transfers between devices  20.6 us (27%)
  Pallas kernels  18.3 us (24%)
  local copies, waits for them, and re-layouts  0.9 us (1%)
    ppermute x7, waiting for transfers between devices, exchanged(): return lax.ppermute(value, ('z', 'y', 'core', 'x'), moves)  15.6 us
    ppermute x7, starting transfers between devices, exchanged(): return lax.ppermute(value, ('z', 'y', 'core', 'x'), moves)  15.3 us
    ppermute x2, starting transfers between devices, other_core(): return lax.ppermute(value, 'core', [(0, 1), (1, 0)])  10.2 us
    ppermute x6, starting transfers between devices, shifted(): return lax.ppermute(value, 'x', [(i, (i + shift) % 4) for i in range(4)])  9.61 us
    pallas_call x1, Pallas kernels, factor_and_scores(): pl.pallas_call(factor_kernel, out_shape=(jax.ShapeDtypeStruct((PART, PROB...  9.09 us
    pallas_call x1, Pallas kernels, project(): pl.pallas_call(project_kernel, out_shape=(piece,) * 4, in_specs=[anywhere...  8.79 us
    ppermute x6, waiting for transfers between devices, shifted(): return lax.ppermute(value, 'x', [(i, (i + shift) % 4) for i in range(4)])  3.15 us
    ppermute x2, waiting for transfers between devices, other_core(): return lax.ppermute(value, 'core', [(0, 1), (1, 0)])  1.89 us
  transfers between devices with their start and end apart: 15, of which 9 were waited for; matrix products, arithmetic and copies ran while one was open for 0% of the time, Pallas kernels for 0%

profile of v3, /device:TPU:1, one launch (start us, length us, event | category | flops | bytes accessed | tf_op | source)
XLA Modules:
  0.0 75.6 jit_solution(13497089513309536861)
XLA Ops:
  0.6 8.8 %project.1 = (f32[112,256]{1,0:T(8,128)}, f32[112,256]{1,0:T(8,128)}, f32[112,256]{1,0:T(8,128)}, f32[112,256]{1,0:T(8,128)}) custom-call(s32[1,448]{1,0:T(1,128)} %bitcast.4, s32[1,448]{1,0:T(1,128)} %bitcast.5, bf16[448,6400]{1,0:T(8,128)(2,1)} %images_ref.1, bf16[2,6400,256]{2,1,0:T(8,128)(2,1)} %panels_ref.1, f32[2,6400]{1,0:T(2,128)} %mean_ref.1, ...), custom_call_target="tpu_custom_call" | custom-call | tf_op jit(solution)/shard_map/project/pallas_call | solution.py:102
  9.4 2.1 %collective-permute-start = (f32[112,256]{1,0:T(8,128)}, f32[112,256]{1,0:T(8,128)S(1)}, u32[]{:S(2)}, u32[]{:S(2)}) collective-permute-start(f32[112,256]{1,0:T(8,128)} %get-tuple-element.16), channel_id=1, source_target_pairs={{0,1},{1,2},{2,3},{3,0},{4,5},{5,6},{6,7},{7,4},{8,9},{9,10},{10,1... | collective-permute-start | bytes 344072 | tf_op jit(solution)/shard_map/ppermute | solution.py:289
  11.6 2.5 %collective-permute-start.1 = (f32[112,256]{1,0:T(8,128)}, f32[112,256]{1,0:T(8,128)S(1)}, u32[]{:S(2)}, u32[]{:S(2)}) collective-permute-start(f32[112,256]{1,0:T(8,128)} %get-tuple-element.17), channel_id=1, source_target_pairs={{0,2},{1,3},{2,0},{3,1},{4,6},{5,7},{6,4},{7,5},{8,10},{9,11},{10,... | collective-permute-start | bytes 344072 | tf_op jit(solution)/shard_map/ppermute | solution.py:289
  14.0 1.2 %collective-permute-start.2 = (f32[112,256]{1,0:T(8,128)}, f32[112,256]{1,0:T(8,128)S(1)}, u32[]{:S(2)}, u32[]{:S(2)}) collective-permute-start(f32[112,256]{1,0:T(8,128)} %get-tuple-element.18), channel_id=1, source_target_pairs={{0,3},{1,0},{2,1},{3,2},{4,7},{5,4},{6,5},{7,6},{8,11},{9,8},{10,9... | collective-permute-start | bytes 344072 | tf_op jit(solution)/shard_map/ppermute | solution.py:289
  16.1 3.1 %collective-permute-done.1.second_ref = f32[112,256]{1,0:T(8,128)S(1)} collective-permute-done((f32[112,256]{1,0:T(8,128)}, f32[112,256]{1,0:T(8,128)S(1)}, u32[]{:S(2)}, u32[]{:S(2)}) %collective-permute-start.1) | collective-permute-done | bytes 114720 | tf_op jit(solution)/shard_map/ppermute | solution.py:289
  19.6 2.0 %collective-permute-start.3 = (f32[192,128]{1,0:T(8,128)S(1)}, f32[192,128]{1,0:T(8,128)S(1)}, u32[]{:S(2)}, u32[]{:S(2)}) collective-permute-start(f32[192,128]{1,0:T(8,128)S(1)} %get-tuple-element.20), channel_id=1, source_target_pairs={{0,4},{4,0},{1,5},{5,1},{2,6},{6,2},{3,7},{7,3},{8,12},{12,8},{9,1... | collective-permute-start | bytes 294920 | tf_op jit(solution)/shard_map/ppermute | solution.py:312
  21.6 0.9 %collective-permute-done.3 = f32[192,128]{1,0:T(8,128)S(1)} collective-permute-done((f32[192,128]{1,0:T(8,128)S(1)}, f32[192,128]{1,0:T(8,128)S(1)}, u32[]{:S(2)}, u32[]{:S(2)}) %collective-permute-start.3) | collective-permute-done | bytes 98336 | tf_op jit(solution)/shard_map/ppermute | solution.py:312
  22.6 1.0 %collective-permute-start.4 = (f32[192,128]{1,0:T(8,128)S(1)}, f32[192,128]{1,0:T(8,128)S(1)}, u32[]{:S(2)}, u32[]{:S(2)}) collective-permute-start(f32[192,128]{1,0:T(8,128)S(1)} %add.24), channel_id=1, source_target_pairs={{0,1},{1,0},{2,3},{3,2},{4,12},{5,13},{6,14},{7,15},{8,9},{9,8},{1... | collective-permute-start | bytes 294920 | tf_op jit(solution)/shard_map/ppermute | solution.py:308
  23.6 2.8 %collective-permute-done.4 = f32[192,128]{1,0:T(8,128)S(1)} collective-permute-done((f32[192,128]{1,0:T(8,128)S(1)}, f32[192,128]{1,0:T(8,128)S(1)}, u32[]{:S(2)}, u32[]{:S(2)}) %collective-permute-start.4) | collective-permute-done | bytes 98336 | tf_op jit(solution)/shard_map/ppermute | solution.py:308
  26.4 2.5 %collective-permute-start.5 = (f32[192,128]{1,0:T(8,128)S(1)}, f32[192,128]{1,0:T(8,128)S(1)}, u32[]{:S(2)}, u32[]{:S(2)}) collective-permute-start(f32[192,128]{1,0:T(8,128)S(1)} %add.25), channel_id=1, source_target_pairs={{0,3},{1,2},{2,1},{3,0},{4,28},{5,29},{6,30},{7,31},{8,11},{9,10},... | collective-permute-start | bytes 294920 | tf_op jit(solution)/shard_map/ppermute | solution.py:308
  28.9 2.3 %collective-permute-done.5 = f32[192,128]{1,0:T(8,128)S(1)} collective-permute-done((f32[192,128]{1,0:T(8,128)S(1)}, f32[192,128]{1,0:T(8,128)S(1)}, u32[]{:S(2)}, u32[]{:S(2)}) %collective-permute-start.5) | collective-permute-done | bytes 98336 | tf_op jit(solution)/shard_map/ppermute | solution.py:308
  31.2 1.1 %collective-permute-start.6 = (f32[192,128]{1,0:T(8,128)S(1)}, f32[192,128]{1,0:T(8,128)S(1)}, u32[]{:S(2)}, u32[]{:S(2)}) collective-permute-start(f32[192,128]{1,0:T(8,128)S(1)} %add.26), channel_id=1, source_target_pairs={{0,8},{1,9},{2,10},{3,11},{4,5},{5,4},{6,7},{7,6},{8,0},{9,1},{10,... | collective-permute-start | bytes 294920 | tf_op jit(solution)/shard_map/ppermute | solution.py:308
  32.3 2.5 %collective-permute-done.6 = f32[192,128]{1,0:T(8,128)S(1)} collective-permute-done((f32[192,128]{1,0:T(8,128)S(1)}, f32[192,128]{1,0:T(8,128)S(1)}, u32[]{:S(2)}, u32[]{:S(2)}) %collective-permute-start.6) | collective-permute-done | bytes 98336 | tf_op jit(solution)/shard_map/ppermute | solution.py:308
  34.8 2.4 %collective-permute-start.7 = (f32[192,128]{1,0:T(8,128)S(1)}, f32[192,128]{1,0:T(8,128)S(1)}, u32[]{:S(2)}, u32[]{:S(2)}) collective-permute-start(f32[192,128]{1,0:T(8,128)S(1)} %add.27), channel_id=1, source_target_pairs={{0,24},{1,25},{2,26},{3,27},{4,7},{5,6},{6,5},{7,4},{8,16},{9,17},... | collective-permute-start | bytes 294920 | tf_op jit(solution)/shard_map/ppermute | solution.py:308
  37.7 2.3 %collective-permute-done.7 = f32[192,128]{1,0:T(8,128)S(1)} collective-permute-done((f32[192,128]{1,0:T(8,128)S(1)}, f32[192,128]{1,0:T(8,128)S(1)}, u32[]{:S(2)}, u32[]{:S(2)}) %collective-permute-start.7) | collective-permute-done | bytes 98336 | tf_op jit(solution)/shard_map/ppermute | solution.py:308
  40.0 1.0 %collective-permute-start.8 = (f32[192,128]{1,0:T(8,128)S(1)}, f32[192,128]{1,0:T(8,128)S(1)}, u32[]{:S(2)}, u32[]{:S(2)}) collective-permute-start(f32[192,128]{1,0:T(8,128)S(1)} %add.28), channel_id=1, source_target_pairs={{0,32},{1,33},{2,34},{3,35},{4,36},{5,37},{6,38},{7,39},{8,40},{9,... | collective-permute-start | bytes 294920 | tf_op jit(solution)/shard_map/ppermute | solution.py:308
  41.0 3.4 %collective-permute-start.11 = (f32[112,256]{1,0:T(8,128)S(1)}, f32[112,256]{1,0:T(8,128)S(1)}, u32[]{:S(2)}, u32[]{:S(2)}) collective-permute-start(f32[112,256]{1,0:T(8,128)S(1)} %get-tuple-element.21.c0_ref), channel_id=1, source_target_pairs={{0,3},{1,0},{2,1},{3,2},{4,7},{5,4},{6,5},{7,6},{8,11},{9,8},{10,9... | collective-permute-start | bytes 344072 | tf_op jit(solution)/shard_map/ppermute | solution.py:289
  44.4 3.1 %collective-permute-start.10 = (f32[192,128]{1,0:T(8,128)S(1)}, f32[192,128]{1,0:T(8,128)S(1)}, u32[]{:S(2)}, u32[]{:S(2)}) collective-permute-start(f32[192,128]{1,0:T(8,128)S(1)} %add.29), channel_id=1, source_target_pairs={{0,64},{1,65},{2,66},{3,67},{4,68},{5,69},{6,70},{7,71},{8,72},{9,... | collective-permute-start | bytes 294920 | tf_op jit(solution)/shard_map/ppermute | solution.py:308
  47.5 3.1 %collective-permute-done.10 = f32[192,128]{1,0:T(8,128)S(1)} collective-permute-done((f32[192,128]{1,0:T(8,128)S(1)}, f32[192,128]{1,0:T(8,128)S(1)}, u32[]{:S(2)}, u32[]{:S(2)}) %collective-permute-start.10) | collective-permute-done | bytes 98336 | tf_op jit(solution)/shard_map/ppermute | solution.py:308
  50.6 4.3 %collective-permute-start.12 = (f32[192,128]{1,0:T(8,128)S(1)}, f32[192,128]{1,0:T(8,128)S(1)}, u32[]{:S(2)}, u32[]{:S(2)}) collective-permute-start(f32[192,128]{1,0:T(8,128)S(1)} %add.30), channel_id=1, source_target_pairs={{0,192},{1,193},{2,194},{3,195},{4,196},{5,197},{6,198},{7,199},{8... | collective-permute-start | bytes 294920 | tf_op jit(solution)/shard_map/ppermute | solution.py:308
  54.8 2.6 %collective-permute-done.12 = f32[192,128]{1,0:T(8,128)S(1)} collective-permute-done((f32[192,128]{1,0:T(8,128)S(1)}, f32[192,128]{1,0:T(8,128)S(1)}, u32[]{:S(2)}, u32[]{:S(2)}) %collective-permute-start.12) | collective-permute-done | bytes 98336 | tf_op jit(solution)/shard_map/ppermute | solution.py:308
  57.5 8.1 %collective-permute-start.14 = (f32[192,128]{1,0:T(8,128)S(1)}, f32[192,128]{1,0:T(8,128)S(1)}, u32[]{:S(2)}, u32[]{:S(2)}) collective-permute-start(f32[192,128]{1,0:T(8,128)S(1)} %add.31.mine_ref), channel_id=1, source_target_pairs={{0,4},{4,0},{1,5},{5,1},{2,6},{6,2},{3,7},{7,3},{8,12},{12,8},{9,1... | collective-permute-start | bytes 294920 | tf_op jit(solution)/shard_map/ppermute | solution.py:312
  65.6 0.9 %collective-permute-done.14.other_ref = f32[192,128]{1,0:T(8,128)S(1)} collective-permute-done((f32[192,128]{1,0:T(8,128)S(1)}, f32[192,128]{1,0:T(8,128)S(1)}, u32[]{:S(2)}, u32[]{:S(2)}) %collective-permute-start.14) | collective-permute-done | bytes 98336 | tf_op jit(solution)/shard_map/ppermute | solution.py:312
  66.6 9.1 %factor.1 = (f32[448,256]{1,0:T(8,128)}, f32[256,256]{1,0:T(8,128)}) custom-call(s32[1]{0:T(128)} %bitcast.place_ref, s32[1]{0:T(128)} %bitcast.1.core_ref, f32[192,128]{1,0:T(8,128)S(1)} %add.31.mine_ref, f32[192,128]{1,0:T(8,128)S(1)} %collective-permute-done.14.other_ref, f32[112,256]{1,0:T(8,128)S(1)} %get-tuple-element.21.c0_ref, ...), custom_call_target="tpu_custom_call" | custom-call | tf_op jit(solution)/shard_map/factor/pallas_call | solution.py:274
  (20 shorter events, 1.9 us)
Async XLA Ops:
  9.4 6.6 %collective-permute-start = (f32[112,256]{1,0:T(8,128)}, f32[112,256]{1,0:T(8,128)S(1)}, u32[]{:S(2)}, u32[]{:S(2)}) collective-permute-start(f32[112,256]{1,0:T(8,128)} %get-tuple-element.16), channel_id=1, source_target_pairs={{0,1},{1,2},{2,3},{3,0},{4,5},{5,6},{6,7},{7,4},{8,9},{9,10},{10,1... | collective-permute-start | bytes 344072 | tf_op jit(solution)/shard_map/ppermute | solution.py:289
  11.6 7.7 %collective-permute-start.1 = (f32[112,256]{1,0:T(8,128)}, f32[112,256]{1,0:T(8,128)S(1)}, u32[]{:S(2)}, u32[]{:S(2)}) collective-permute-start(f32[112,256]{1,0:T(8,128)} %get-tuple-element.17), channel_id=1, source_target_pairs={{0,2},{1,3},{2,0},{3,1},{4,6},{5,7},{6,4},{7,5},{8,10},{9,11},{10,... | collective-permute-start | bytes 344072 | tf_op jit(solution)/shard_map/ppermute | solution.py:289
  14.0 5.2 %collective-permute-start.2 = (f32[112,256]{1,0:T(8,128)}, f32[112,256]{1,0:T(8,128)S(1)}, u32[]{:S(2)}, u32[]{:S(2)}) collective-permute-start(f32[112,256]{1,0:T(8,128)} %get-tuple-element.18), channel_id=1, source_target_pairs={{0,3},{1,0},{2,1},{3,2},{4,7},{5,4},{6,5},{7,6},{8,11},{9,8},{10,9... | collective-permute-start | bytes 344072 | tf_op jit(solution)/shard_map/ppermute | solution.py:289
  15.2 0.9 %copy-start = (f32[112,256]{1,0:T(8,128)S(1)}, f32[112,256]{1,0:T(8,128)}, u32[]{:S(2)}) copy-start(f32[112,256]{1,0:T(8,128)} %get-tuple-element.15.piece_ref) | copy-start | bytes 344068
  19.6 3.0 %collective-permute-start.3 = (f32[192,128]{1,0:T(8,128)S(1)}, f32[192,128]{1,0:T(8,128)S(1)}, u32[]{:S(2)}, u32[]{:S(2)}) collective-permute-start(f32[192,128]{1,0:T(8,128)S(1)} %get-tuple-element.20), channel_id=1, source_target_pairs={{0,4},{4,0},{1,5},{5,1},{2,6},{6,2},{3,7},{7,3},{8,12},{12,8},{9,1... | collective-permute-start | bytes 294920 | tf_op jit(solution)/shard_map/ppermute | solution.py:312
  22.6 3.8 %collective-permute-start.4 = (f32[192,128]{1,0:T(8,128)S(1)}, f32[192,128]{1,0:T(8,128)S(1)}, u32[]{:S(2)}, u32[]{:S(2)}) collective-permute-start(f32[192,128]{1,0:T(8,128)S(1)} %add.24), channel_id=1, source_target_pairs={{0,1},{1,0},{2,3},{3,2},{4,12},{5,13},{6,14},{7,15},{8,9},{9,8},{1... | collective-permute-start | bytes 294920 | tf_op jit(solution)/shard_map/ppermute | solution.py:308
  26.4 4.8 %collective-permute-start.5 = (f32[192,128]{1,0:T(8,128)S(1)}, f32[192,128]{1,0:T(8,128)S(1)}, u32[]{:S(2)}, u32[]{:S(2)}) collective-permute-start(f32[192,128]{1,0:T(8,128)S(1)} %add.25), channel_id=1, source_target_pairs={{0,3},{1,2},{2,1},{3,0},{4,28},{5,29},{6,30},{7,31},{8,11},{9,10},... | collective-permute-start | bytes 294920 | tf_op jit(solution)/shard_map/ppermute | solution.py:308
  31.2 3.6 %collective-permute-start.6 = (f32[192,128]{1,0:T(8,128)S(1)}, f32[192,128]{1,0:T(8,128)S(1)}, u32[]{:S(2)}, u32[]{:S(2)}) collective-permute-start(f32[192,128]{1,0:T(8,128)S(1)} %add.26), channel_id=1, source_target_pairs={{0,8},{1,9},{2,10},{3,11},{4,5},{5,4},{6,7},{7,6},{8,0},{9,1},{10,... | collective-permute-start | bytes 294920 | tf_op jit(solution)/shard_map/ppermute | solution.py:308
  34.8 5.2 %collective-permute-start.7 = (f32[192,128]{1,0:T(8,128)S(1)}, f32[192,128]{1,0:T(8,128)S(1)}, u32[]{:S(2)}, u32[]{:S(2)}) collective-permute-start(f32[192,128]{1,0:T(8,128)S(1)} %add.27), channel_id=1, source_target_pairs={{0,24},{1,25},{2,26},{3,27},{4,7},{5,6},{6,5},{7,4},{8,16},{9,17},... | collective-permute-start | bytes 294920 | tf_op jit(solution)/shard_map/ppermute | solution.py:308
  37.2 7.2 %collective-permute-start.9 = (f32[112,256]{1,0:T(8,128)S(1)}, f32[112,256]{1,0:T(8,128)S(1)}, u32[]{:S(2)}, u32[]{:S(2)}) collective-permute-start(f32[112,256]{1,0:T(8,128)S(1)} %get-tuple-element.21.c0_ref), channel_id=1, source_target_pairs={{0,2},{1,3},{2,0},{3,1},{4,6},{5,7},{6,4},{7,5},{8,10},{9,11},{10,... | collective-permute-start | bytes 344072 | tf_op jit(solution)/shard_map/ppermute | solution.py:289
  40.0 4.4 %collective-permute-start.8 = (f32[192,128]{1,0:T(8,128)S(1)}, f32[192,128]{1,0:T(8,128)S(1)}, u32[]{:S(2)}, u32[]{:S(2)}) collective-permute-start(f32[192,128]{1,0:T(8,128)S(1)} %add.28), channel_id=1, source_target_pairs={{0,32},{1,33},{2,34},{3,35},{4,36},{5,37},{6,38},{7,39},{8,40},{9,... | collective-permute-start | bytes 294920 | tf_op jit(solution)/shard_map/ppermute | solution.py:308
  41.0 9.6 %collective-permute-start.11 = (f32[112,256]{1,0:T(8,128)S(1)}, f32[112,256]{1,0:T(8,128)S(1)}, u32[]{:S(2)}, u32[]{:S(2)}) collective-permute-start(f32[112,256]{1,0:T(8,128)S(1)} %get-tuple-element.21.c0_ref), channel_id=1, source_target_pairs={{0,3},{1,0},{2,1},{3,2},{4,7},{5,4},{6,5},{7,6},{8,11},{9,8},{10,9... | collective-permute-start | bytes 344072 | tf_op jit(solution)/shard_map/ppermute | solution.py:289
  44.4 6.1 %collective-permute-start.10 = (f32[192,128]{1,0:T(8,128)S(1)}, f32[192,128]{1,0:T(8,128)S(1)}, u32[]{:S(2)}, u32[]{:S(2)}) collective-permute-start(f32[192,128]{1,0:T(8,128)S(1)} %add.29), channel_id=1, source_target_pairs={{0,64},{1,65},{2,66},{3,67},{4,68},{5,69},{6,70},{7,71},{8,72},{9,... | collective-permute-start | bytes 294920 | tf_op jit(solution)/shard_map/ppermute | solution.py:308
  47.5 10.0 %collective-permute-start.13 = (f32[112,256]{1,0:T(8,128)S(1)}, f32[112,256]{1,0:T(8,128)S(1)}, u32[]{:S(2)}, u32[]{:S(2)}) collective-permute-start(f32[112,256]{1,0:T(8,128)S(1)} %get-tuple-element.21.c0_ref), channel_id=1, source_target_pairs={{0,1},{1,2},{2,3},{3,0},{4,5},{5,6},{6,7},{7,4},{8,9},{9,10},{10,1... | collective-permute-start | bytes 344072 | tf_op jit(solution)/shard_map/ppermute | solution.py:289
  50.6 6.9 %collective-permute-start.12 = (f32[192,128]{1,0:T(8,128)S(1)}, f32[192,128]{1,0:T(8,128)S(1)}, u32[]{:S(2)}, u32[]{:S(2)}) collective-permute-start(f32[192,128]{1,0:T(8,128)S(1)} %add.30), channel_id=1, source_target_pairs={{0,192},{1,193},{2,194},{3,195},{4,196},{5,197},{6,198},{7,199},{8... | collective-permute-start | bytes 294920 | tf_op jit(solution)/shard_map/ppermute | solution.py:308
  57.5 9.1 %collective-permute-start.14 = (f32[192,128]{1,0:T(8,128)S(1)}, f32[192,128]{1,0:T(8,128)S(1)}, u32[]{:S(2)}, u32[]{:S(2)}) collective-permute-start(f32[192,128]{1,0:T(8,128)S(1)} %add.31.mine_ref), channel_id=1, source_target_pairs={{0,4},{4,0},{1,5},{5,1},{2,6},{6,2},{3,7},{7,3},{8,12},{12,8},{9,1... | collective-permute-start | bytes 294920 | tf_op jit(solution)/shard_map/ppermute | solution.py:312

commit v4 on v3

--- a/solution.py
+++ b/solution.py
@@ -18,7 +18,7 @@
 STEP = 1280
 GROUPS = 16
 PROBES = 256
-HALF = 192
+HALF = 136
 
 
 def three_terms(value):
@@ -149,10 +149,14 @@
         )
         return gram / particles
 
+    lane = lax.broadcasted_iota(jnp.int32, (128, 128), 1)
+    row = lax.broadcasted_iota(jnp.int32, (128, 128), 0)
     top = block(coeffs[:, :128], coeffs)
-    packed[:128, :] = top[:, :128]
-    packed[128:256, :] = top[:, 128:]
-    packed[256:, :] = block(coeffs[:, 128:], coeffs[:, 128:])
+    bottom = block(coeffs[:, 128:], coeffs[:, 128:])
+    diagonal = jnp.sum(jnp.where(row == lane, bottom, 0.0), axis=0, keepdims=True)
+    packed[:128, :] = top[:, 128:]
+    packed[128:256, :] = jnp.where(row >= lane, top[:, :128], bottom)
+    packed[256:, :] = jnp.broadcast_to(diagonal, (16, 128))
     core = core_ref[0]
     mine_ref[...] = packed[pl.ds(pl.multiple_of(core * HALF, 8), HALF), :]
     other_ref[...] = packed[pl.ds(pl.multiple_of((1 - core) * HALF, 8), HALF), :]
@@ -176,13 +180,19 @@
 
 
 def factor_kernel(
-    place_ref, core_ref, mine_ref, other_ref, c0_ref, c1_ref, c2_ref, c3_ref, scores_ref, factor_ref, work, inv
+    place_ref, core_ref, mine_ref, other_ref, c0_ref, c1_ref, c2_ref, c3_ref, scores_ref, factor_ref, packed, work, inv
 ):
     lane = lax.broadcasted_iota(jnp.int32, (256, 256), 1)
     row = lax.broadcasted_iota(jnp.int32, (256, 256), 0)
     core = core_ref[0]
-    work[pl.ds(pl.multiple_of(core * HALF, 8), HALF), :] = mine_ref[...]
-    work[pl.ds(pl.multiple_of((1 - core) * HALF, 8), HALF), :] = other_ref[...]
+    packed[pl.ds(pl.multiple_of(core * HALF, 8), HALF), :] = mine_ref[...]
+    packed[pl.ds(pl.multiple_of((1 - core) * HALF, 8), HALF), :] = other_ref[...]
+    below = row[:128, :128] - lane[:128, :128]
+    halves = packed[128:256, :]
+    turned = halves.T
+    work[:128, :] = jnp.where(below >= 0, halves, turned)
+    work[128:256, :] = packed[:128, :]
+    work[256:, :] = jnp.where(below < 0, halves, jnp.where(below > 0, turned, packed[256:257, :]))
     inv[...] = jnp.where(lane == row, 1.0, 0.0).astype(F32)
     sub = lax.broadcasted_iota(jnp.int32, (8, 128), 0)
 
@@ -279,7 +289,11 @@
         ),
         in_specs=[pl.BlockSpec(memory_space=pltpu.SMEM)] * 2 + [vmem] * 6,
         out_specs=(vmem, vmem),
-        scratch_shapes=[pltpu.VMEM((2 * HALF, 128), F32), pltpu.VMEM((PROBES, PROBES), F32)],
+        scratch_shapes=[
+            pltpu.VMEM((2 * HALF, 128), F32),
+            pltpu.VMEM((384, 128), F32),
+            pltpu.VMEM((PROBES, PROBES), F32),
+        ],
         compiler_params=pltpu.CompilerParams(vmem_limit_bytes=12 * 1024 * 1024),
         name="factor",
     )(place, core, *halves, *pieces)

time: 75.8 us -> 71.8 us (0.947)
  waiting for transfers between devices: 20.6 us -> 16.6 us
    ppermute x7, waiting for transfers between devices: 15.6 us -> 11.6 us  [exchanged(): return lax.ppermute(value, ('z', 'y', 'core', 'x'), moves)]
    ppermute x6, starting transfers between devices: 9.61 us -> 8.38 us  [shifted(): return lax.ppermute(value, 'x', [(i, (i + shift) % 4) for i in range(4)])]
    ppermute x7, starting transfers between devices: 15.3 us -> 16.4 us  [exchanged(): return lax.ppermute(value, ('z', 'y', 'core', 'x'), moves)]
where the time goes in v4:
time: 71.8 us; the launch traced here: 71.7 us
  starting transfers between devices  35.1 us (49%)
  Pallas kernels  18.3 us (25%)
  waiting for transfers between devices  16.6 us (23%)
  local copies, waits for them, and re-layouts  0.9 us (1%)
  between operations  0.72 us (1%)
    ppermute x7, starting transfers between devices, exchanged(): return lax.ppermute(value, ('z', 'y', 'core', 'x'), moves)  16.4 us
    ppermute x7, waiting for transfers between devices, exchanged(): return lax.ppermute(value, ('z', 'y', 'core', 'x'), moves)  11.6 us
    ppermute x2, starting transfers between devices, other_core(): return lax.ppermute(value, 'core', [(0, 1), (1, 0)])  10.3 us
    pallas_call x1, Pallas kernels, factor_and_scores(): pl.pallas_call(factor_kernel, out_shape=(jax.ShapeDtypeStruct((PART, PROB...  9.13 us
    pallas_call x1, Pallas kernels, project(): pl.pallas_call(project_kernel, out_shape=(piece,) * 4, in_specs=[anywhere...  8.79 us
    ppermute x6, starting transfers between devices, shifted(): return lax.ppermute(value, 'x', [(i, (i + shift) % 4) for i in range(4)])  8.38 us
    ppermute x6, waiting for transfers between devices, shifted(): return lax.ppermute(value, 'x', [(i, (i + shift) % 4) for i in range(4)])  3.15 us
    ppermute x2, waiting for transfers between devices, other_core(): return lax.ppermute(value, 'core', [(0, 1), (1, 0)])  1.81 us
  transfers between devices with their start and end apart: 15, of which 9 were waited for; matrix products, arithmetic and copies ran while one was open for 0% of the time, Pallas kernels for 0%

profile of v4, /device:TPU:1, one launch (start us, length us, event | category | flops | bytes accessed | tf_op | source)
XLA Modules:
  0.0 71.7 jit_solution(13098824899608263108)
XLA Ops:
  0.6 8.8 %project.1 = (f32[112,256]{1,0:T(8,128)}, f32[112,256]{1,0:T(8,128)}, f32[112,256]{1,0:T(8,128)}, f32[112,256]{1,0:T(8,128)}) custom-call(s32[1,448]{1,0:T(1,128)} %bitcast.4, s32[1,448]{1,0:T(1,128)} %bitcast.5, bf16[448,6400]{1,0:T(8,128)(2,1)} %images_ref.1, bf16[2,6400,256]{2,1,0:T(8,128)(2,1)} %panels_ref.1, f32[2,6400]{1,0:T(2,128)} %mean_ref.1, ...), custom_call_target="tpu_custom_call" | custom-call | tf_op jit(solution)/shard_map/project/pallas_call | solution.py:102
  9.4 2.1 %collective-permute-start = (f32[112,256]{1,0:T(8,128)}, f32[112,256]{1,0:T(8,128)S(1)}, u32[]{:S(2)}, u32[]{:S(2)}) collective-permute-start(f32[112,256]{1,0:T(8,128)} %get-tuple-element.16), channel_id=1, source_target_pairs={{0,1},{1,2},{2,3},{3,0},{4,5},{5,6},{6,7},{7,4},{8,9},{9,10},{10,1... | collective-permute-start | bytes 344072 | tf_op jit(solution)/shard_map/ppermute | solution.py:303
  11.6 2.5 %collective-permute-start.1 = (f32[112,256]{1,0:T(8,128)}, f32[112,256]{1,0:T(8,128)S(1)}, u32[]{:S(2)}, u32[]{:S(2)}) collective-permute-start(f32[112,256]{1,0:T(8,128)} %get-tuple-element.17), channel_id=1, source_target_pairs={{0,2},{1,3},{2,0},{3,1},{4,6},{5,7},{6,4},{7,5},{8,10},{9,11},{10,... | collective-permute-start | bytes 344072 | tf_op jit(solution)/shard_map/ppermute | solution.py:303
  14.0 1.2 %collective-permute-start.2 = (f32[112,256]{1,0:T(8,128)}, f32[112,256]{1,0:T(8,128)S(1)}, u32[]{:S(2)}, u32[]{:S(2)}) collective-permute-start(f32[112,256]{1,0:T(8,128)} %get-tuple-element.18), channel_id=1, source_target_pairs={{0,3},{1,0},{2,1},{3,2},{4,7},{5,4},{6,5},{7,6},{8,11},{9,8},{10,9... | collective-permute-start | bytes 344072 | tf_op jit(solution)/shard_map/ppermute | solution.py:303
  16.1 3.1 %collective-permute-done.1.second_ref = f32[112,256]{1,0:T(8,128)S(1)} collective-permute-done((f32[112,256]{1,0:T(8,128)}, f32[112,256]{1,0:T(8,128)S(1)}, u32[]{:S(2)}, u32[]{:S(2)}) %collective-permute-start.1) | collective-permute-done | bytes 114720 | tf_op jit(solution)/shard_map/ppermute | solution.py:303
  19.6 2.0 %collective-permute-start.3 = (f32[136,128]{1,0:T(8,128)S(1)}, f32[136,128]{1,0:T(8,128)S(1)}, u32[]{:S(2)}, u32[]{:S(2)}) collective-permute-start(f32[136,128]{1,0:T(8,128)S(1)} %get-tuple-element.20), channel_id=1, source_target_pairs={{0,4},{4,0},{1,5},{5,1},{2,6},{6,2},{3,7},{7,3},{8,12},{12,8},{9,1... | collective-permute-start | bytes 208904 | tf_op jit(solution)/shard_map/ppermute | solution.py:326
  21.6 0.9 %collective-permute-done.3 = f32[136,128]{1,0:T(8,128)S(1)} collective-permute-done((f32[136,128]{1,0:T(8,128)S(1)}, f32[136,128]{1,0:T(8,128)S(1)}, u32[]{:S(2)}, u32[]{:S(2)}) %collective-permute-start.3) | collective-permute-done | bytes 69664 | tf_op jit(solution)/shard_map/ppermute | solution.py:326
  22.5 1.0 %collective-permute-start.4 = (f32[136,128]{1,0:T(8,128)S(1)}, f32[136,128]{1,0:T(8,128)S(1)}, u32[]{:S(2)}, u32[]{:S(2)}) collective-permute-start(f32[136,128]{1,0:T(8,128)S(1)} %add.24), channel_id=1, source_target_pairs={{0,1},{1,0},{2,3},{3,2},{4,12},{5,13},{6,14},{7,15},{8,9},{9,8},{1... | collective-permute-start | bytes 208904 | tf_op jit(solution)/shard_map/ppermute | solution.py:322
  23.6 2.2 %collective-permute-done.4 = f32[136,128]{1,0:T(8,128)S(1)} collective-permute-done((f32[136,128]{1,0:T(8,128)S(1)}, f32[136,128]{1,0:T(8,128)S(1)}, u32[]{:S(2)}, u32[]{:S(2)}) %collective-permute-start.4) | collective-permute-done | bytes 69664 | tf_op jit(solution)/shard_map/ppermute | solution.py:322
  25.8 2.5 %collective-permute-start.5 = (f32[136,128]{1,0:T(8,128)S(1)}, f32[136,128]{1,0:T(8,128)S(1)}, u32[]{:S(2)}, u32[]{:S(2)}) collective-permute-start(f32[136,128]{1,0:T(8,128)S(1)} %add.25), channel_id=1, source_target_pairs={{0,3},{1,2},{2,1},{3,0},{4,28},{5,29},{6,30},{7,31},{8,11},{9,10},... | collective-permute-start | bytes 208904 | tf_op jit(solution)/shard_map/ppermute | solution.py:322
  28.2 2.0 %collective-permute-done.5 = f32[136,128]{1,0:T(8,128)S(1)} collective-permute-done((f32[136,128]{1,0:T(8,128)S(1)}, f32[136,128]{1,0:T(8,128)S(1)}, u32[]{:S(2)}, u32[]{:S(2)}) %collective-permute-start.5) | collective-permute-done | bytes 69664 | tf_op jit(solution)/shard_map/ppermute | solution.py:322
  30.3 1.1 %collective-permute-start.6 = (f32[136,128]{1,0:T(8,128)S(1)}, f32[136,128]{1,0:T(8,128)S(1)}, u32[]{:S(2)}, u32[]{:S(2)}) collective-permute-start(f32[136,128]{1,0:T(8,128)S(1)} %add.26), channel_id=1, source_target_pairs={{0,8},{1,9},{2,10},{3,11},{4,5},{5,4},{6,7},{7,6},{8,0},{9,1},{10,... | collective-permute-start | bytes 208904 | tf_op jit(solution)/shard_map/ppermute | solution.py:322
  31.4 2.1 %collective-permute-done.6 = f32[136,128]{1,0:T(8,128)S(1)} collective-permute-done((f32[136,128]{1,0:T(8,128)S(1)}, f32[136,128]{1,0:T(8,128)S(1)}, u32[]{:S(2)}, u32[]{:S(2)}) %collective-permute-start.6) | collective-permute-done | bytes 69664 | tf_op jit(solution)/shard_map/ppermute | solution.py:322
  33.5 2.4 %collective-permute-start.7 = (f32[136,128]{1,0:T(8,128)S(1)}, f32[136,128]{1,0:T(8,128)S(1)}, u32[]{:S(2)}, u32[]{:S(2)}) collective-permute-start(f32[136,128]{1,0:T(8,128)S(1)} %add.27), channel_id=1, source_target_pairs={{0,24},{1,25},{2,26},{3,27},{4,7},{5,6},{6,5},{7,4},{8,16},{9,17},... | collective-permute-start | bytes 208904 | tf_op jit(solution)/shard_map/ppermute | solution.py:322
  36.4 1.6 %collective-permute-done.7 = f32[136,128]{1,0:T(8,128)S(1)} collective-permute-done((f32[136,128]{1,0:T(8,128)S(1)}, f32[136,128]{1,0:T(8,128)S(1)}, u32[]{:S(2)}, u32[]{:S(2)}) %collective-permute-start.7) | collective-permute-done | bytes 69664 | tf_op jit(solution)/shard_map/ppermute | solution.py:322
  38.0 1.4 %collective-permute-start.8 = (f32[136,128]{1,0:T(8,128)S(1)}, f32[136,128]{1,0:T(8,128)S(1)}, u32[]{:S(2)}, u32[]{:S(2)}) collective-permute-start(f32[136,128]{1,0:T(8,128)S(1)} %add.28), channel_id=1, source_target_pairs={{0,32},{1,33},{2,34},{3,35},{4,36},{5,37},{6,38},{7,39},{8,40},{9,... | collective-permute-start | bytes 208904 | tf_op jit(solution)/shard_map/ppermute | solution.py:322
  39.4 2.2 %collective-permute-start.11 = (f32[112,256]{1,0:T(8,128)S(1)}, f32[112,256]{1,0:T(8,128)S(1)}, u32[]{:S(2)}, u32[]{:S(2)}) collective-permute-start(f32[112,256]{1,0:T(8,128)S(1)} %get-tuple-element.21.c0_ref), channel_id=1, source_target_pairs={{0,3},{1,0},{2,1},{3,2},{4,7},{5,4},{6,5},{7,6},{8,11},{9,8},{10,9... | collective-permute-start | bytes 344072 | tf_op jit(solution)/shard_map/ppermute | solution.py:303
  41.6 3.1 %collective-permute-start.10 = (f32[136,128]{1,0:T(8,128)S(1)}, f32[136,128]{1,0:T(8,128)S(1)}, u32[]{:S(2)}, u32[]{:S(2)}) collective-permute-start(f32[136,128]{1,0:T(8,128)S(1)} %add.29), channel_id=1, source_target_pairs={{0,64},{1,65},{2,66},{3,67},{4,68},{5,69},{6,70},{7,71},{8,72},{9,... | collective-permute-start | bytes 208904 | tf_op jit(solution)/shard_map/ppermute | solution.py:322
  44.7 1.9 %collective-permute-done.10 = f32[136,128]{1,0:T(8,128)S(1)} collective-permute-done((f32[136,128]{1,0:T(8,128)S(1)}, f32[136,128]{1,0:T(8,128)S(1)}, u32[]{:S(2)}, u32[]{:S(2)}) %collective-permute-start.10) | collective-permute-done | bytes 69664 | tf_op jit(solution)/shard_map/ppermute | solution.py:322
  46.6 4.9 %collective-permute-start.12 = (f32[136,128]{1,0:T(8,128)S(1)}, f32[136,128]{1,0:T(8,128)S(1)}, u32[]{:S(2)}, u32[]{:S(2)}) collective-permute-start(f32[136,128]{1,0:T(8,128)S(1)} %add.30), channel_id=1, source_target_pairs={{0,192},{1,193},{2,194},{3,195},{4,196},{5,197},{6,198},{7,199},{8... | collective-permute-start | bytes 208904 | tf_op jit(solution)/shard_map/ppermute | solution.py:322
  51.5 1.8 %collective-permute-done.12 = f32[136,128]{1,0:T(8,128)S(1)} collective-permute-done((f32[136,128]{1,0:T(8,128)S(1)}, f32[136,128]{1,0:T(8,128)S(1)}, u32[]{:S(2)}, u32[]{:S(2)}) %collective-permute-start.12) | collective-permute-done | bytes 69664 | tf_op jit(solution)/shard_map/ppermute | solution.py:322
  53.3 8.3 %collective-permute-start.14 = (f32[136,128]{1,0:T(8,128)S(1)}, f32[136,128]{1,0:T(8,128)S(1)}, u32[]{:S(2)}, u32[]{:S(2)}) collective-permute-start(f32[136,128]{1,0:T(8,128)S(1)} %add.31.mine_ref), channel_id=1, source_target_pairs={{0,4},{4,0},{1,5},{5,1},{2,6},{6,2},{3,7},{7,3},{8,12},{12,8},{9,1... | collective-permute-start | bytes 208904 | tf_op jit(solution)/shard_map/ppermute | solution.py:326
  61.7 0.9 %collective-permute-done.14.other_ref = f32[136,128]{1,0:T(8,128)S(1)} collective-permute-done((f32[136,128]{1,0:T(8,128)S(1)}, f32[136,128]{1,0:T(8,128)S(1)}, u32[]{:S(2)}, u32[]{:S(2)}) %collective-permute-start.14) | collective-permute-done | bytes 69664 | tf_op jit(solution)/shard_map/ppermute | solution.py:326
  62.6 9.1 %factor.1 = (f32[448,256]{1,0:T(8,128)}, f32[256,256]{1,0:T(8,128)}) custom-call(s32[1]{0:T(128)} %bitcast.place_ref, s32[1]{0:T(128)} %bitcast.1.core_ref, f32[136,128]{1,0:T(8,128)S(1)} %add.31.mine_ref, f32[136,128]{1,0:T(8,128)S(1)} %collective-permute-done.14.other_ref, f32[112,256]{1,0:T(8,128)S(1)} %get-tuple-element.21.c0_ref, ...), custom_call_target="tpu_custom_call" | custom-call | tf_op jit(solution)/shard_map/factor/pallas_call | solution.py:284
  (20 shorter events, 1.9 us)
Async XLA Ops:
  9.4 6.6 %collective-permute-start = (f32[112,256]{1,0:T(8,128)}, f32[112,256]{1,0:T(8,128)S(1)}, u32[]{:S(2)}, u32[]{:S(2)}) collective-permute-start(f32[112,256]{1,0:T(8,128)} %get-tuple-element.16), channel_id=1, source_target_pairs={{0,1},{1,2},{2,3},{3,0},{4,5},{5,6},{6,7},{7,4},{8,9},{9,10},{10,1... | collective-permute-start | bytes 344072 | tf_op jit(solution)/shard_map/ppermute | solution.py:303
  11.6 7.7 %collective-permute-start.1 = (f32[112,256]{1,0:T(8,128)}, f32[112,256]{1,0:T(8,128)S(1)}, u32[]{:S(2)}, u32[]{:S(2)}) collective-permute-start(f32[112,256]{1,0:T(8,128)} %get-tuple-element.17), channel_id=1, source_target_pairs={{0,2},{1,3},{2,0},{3,1},{4,6},{5,7},{6,4},{7,5},{8,10},{9,11},{10,... | collective-permute-start | bytes 344072 | tf_op jit(solution)/shard_map/ppermute | solution.py:303
  14.0 5.2 %collective-permute-start.2 = (f32[112,256]{1,0:T(8,128)}, f32[112,256]{1,0:T(8,128)S(1)}, u32[]{:S(2)}, u32[]{:S(2)}) collective-permute-start(f32[112,256]{1,0:T(8,128)} %get-tuple-element.18), channel_id=1, source_target_pairs={{0,3},{1,0},{2,1},{3,2},{4,7},{5,4},{6,5},{7,6},{8,11},{9,8},{10,9... | collective-permute-start | bytes 344072 | tf_op jit(solution)/shard_map/ppermute | solution.py:303
  15.2 0.9 %copy-start = (f32[112,256]{1,0:T(8,128)S(1)}, f32[112,256]{1,0:T(8,128)}, u32[]{:S(2)}) copy-start(f32[112,256]{1,0:T(8,128)} %get-tuple-element.15.piece_ref) | copy-start | bytes 344068
  19.6 2.9 %collective-permute-start.3 = (f32[136,128]{1,0:T(8,128)S(1)}, f32[136,128]{1,0:T(8,128)S(1)}, u32[]{:S(2)}, u32[]{:S(2)}) collective-permute-start(f32[136,128]{1,0:T(8,128)S(1)} %get-tuple-element.20), channel_id=1, source_target_pairs={{0,4},{4,0},{1,5},{5,1},{2,6},{6,2},{3,7},{7,3},{8,12},{12,8},{9,1... | collective-permute-start | bytes 208904 | tf_op jit(solution)/shard_map/ppermute | solution.py:326
  22.5 3.2 %collective-permute-start.4 = (f32[136,128]{1,0:T(8,128)S(1)}, f32[136,128]{1,0:T(8,128)S(1)}, u32[]{:S(2)}, u32[]{:S(2)}) collective-permute-start(f32[136,128]{1,0:T(8,128)S(1)} %add.24), channel_id=1, source_target_pairs={{0,1},{1,0},{2,3},{3,2},{4,12},{5,13},{6,14},{7,15},{8,9},{9,8},{1... | collective-permute-start | bytes 208904 | tf_op jit(solution)/shard_map/ppermute | solution.py:322
  25.8 4.5 %collective-permute-start.5 = (f32[136,128]{1,0:T(8,128)S(1)}, f32[136,128]{1,0:T(8,128)S(1)}, u32[]{:S(2)}, u32[]{:S(2)}) collective-permute-start(f32[136,128]{1,0:T(8,128)S(1)} %add.25), channel_id=1, source_target_pairs={{0,3},{1,2},{2,1},{3,0},{4,28},{5,29},{6,30},{7,31},{8,11},{9,10},... | collective-permute-start | bytes 208904 | tf_op jit(solution)/shard_map/ppermute | solution.py:322
  30.3 3.2 %collective-permute-start.6 = (f32[136,128]{1,0:T(8,128)S(1)}, f32[136,128]{1,0:T(8,128)S(1)}, u32[]{:S(2)}, u32[]{:S(2)}) collective-permute-start(f32[136,128]{1,0:T(8,128)S(1)} %add.26), channel_id=1, source_target_pairs={{0,8},{1,9},{2,10},{3,11},{4,5},{5,4},{6,7},{7,6},{8,0},{9,1},{10,... | collective-permute-start | bytes 208904 | tf_op jit(solution)/shard_map/ppermute | solution.py:322
  33.5 4.5 %collective-permute-start.7 = (f32[136,128]{1,0:T(8,128)S(1)}, f32[136,128]{1,0:T(8,128)S(1)}, u32[]{:S(2)}, u32[]{:S(2)}) collective-permute-start(f32[136,128]{1,0:T(8,128)S(1)} %add.27), channel_id=1, source_target_pairs={{0,24},{1,25},{2,26},{3,27},{4,7},{5,6},{6,5},{7,4},{8,16},{9,17},... | collective-permute-start | bytes 208904 | tf_op jit(solution)/shard_map/ppermute | solution.py:322
  35.9 5.7 %collective-permute-start.9 = (f32[112,256]{1,0:T(8,128)S(1)}, f32[112,256]{1,0:T(8,128)S(1)}, u32[]{:S(2)}, u32[]{:S(2)}) collective-permute-start(f32[112,256]{1,0:T(8,128)S(1)} %get-tuple-element.21.c0_ref), channel_id=1, source_target_pairs={{0,2},{1,3},{2,0},{3,1},{4,6},{5,7},{6,4},{7,5},{8,10},{9,11},{10,... | collective-permute-start | bytes 344072 | tf_op jit(solution)/shard_map/ppermute | solution.py:303
  38.0 3.6 %collective-permute-start.8 = (f32[136,128]{1,0:T(8,128)S(1)}, f32[136,128]{1,0:T(8,128)S(1)}, u32[]{:S(2)}, u32[]{:S(2)}) collective-permute-start(f32[136,128]{1,0:T(8,128)S(1)} %add.28), channel_id=1, source_target_pairs={{0,32},{1,33},{2,34},{3,35},{4,36},{5,37},{6,38},{7,39},{8,40},{9,... | collective-permute-start | bytes 208904 | tf_op jit(solution)/shard_map/ppermute | solution.py:322
  39.4 7.2 %collective-permute-start.11 = (f32[112,256]{1,0:T(8,128)S(1)}, f32[112,256]{1,0:T(8,128)S(1)}, u32[]{:S(2)}, u32[]{:S(2)}) collective-permute-start(f32[112,256]{1,0:T(8,128)S(1)} %get-tuple-element.21.c0_ref), channel_id=1, source_target_pairs={{0,3},{1,0},{2,1},{3,2},{4,7},{5,4},{6,5},{7,6},{8,11},{9,8},{10,9... | collective-permute-start | bytes 344072 | tf_op jit(solution)/shard_map/ppermute | solution.py:303
  41.6 5.0 %collective-permute-start.10 = (f32[136,128]{1,0:T(8,128)S(1)}, f32[136,128]{1,0:T(8,128)S(1)}, u32[]{:S(2)}, u32[]{:S(2)}) collective-permute-start(f32[136,128]{1,0:T(8,128)S(1)} %add.29), channel_id=1, source_target_pairs={{0,64},{1,65},{2,66},{3,67},{4,68},{5,69},{6,70},{7,71},{8,72},{9,... | collective-permute-start | bytes 208904 | tf_op jit(solution)/shard_map/ppermute | solution.py:322
  44.7 8.6 %collective-permute-start.13 = (f32[112,256]{1,0:T(8,128)S(1)}, f32[112,256]{1,0:T(8,128)S(1)}, u32[]{:S(2)}, u32[]{:S(2)}) collective-permute-start(f32[112,256]{1,0:T(8,128)S(1)} %get-tuple-element.21.c0_ref), channel_id=1, source_target_pairs={{0,1},{1,2},{2,3},{3,0},{4,5},{5,6},{6,7},{7,4},{8,9},{9,10},{10,1... | collective-permute-start | bytes 344072 | tf_op jit(solution)/shard_map/ppermute | solution.py:303
  46.6 6.7 %collective-permute-start.12 = (f32[136,128]{1,0:T(8,128)S(1)}, f32[136,128]{1,0:T(8,128)S(1)}, u32[]{:S(2)}, u32[]{:S(2)}) collective-permute-start(f32[136,128]{1,0:T(8,128)S(1)} %add.30), channel_id=1, source_target_pairs={{0,192},{1,193},{2,194},{3,195},{4,196},{5,197},{6,198},{7,199},{8... | collective-permute-start | bytes 208904 | tf_op jit(solution)/shard_map/ppermute | solution.py:322
  53.3 9.2 %collective-permute-start.14 = (f32[136,128]{1,0:T(8,128)S(1)}, f32[136,128]{1,0:T(8,128)S(1)}, u32[]{:S(2)}, u32[]{:S(2)}) collective-permute-start(f32[136,128]{1,0:T(8,128)S(1)} %add.31.mine_ref), channel_id=1, source_target_pairs={{0,4},{4,0},{1,5},{5,1},{2,6},{6,2},{3,7},{7,3},{8,12},{12,8},{9,1... | collective-permute-start | bytes 208904 | tf_op jit(solution)/shard_map/ppermute | solution.py:326

commit v5 on v4

--- a/solution.py
+++ b/solution.py
@@ -180,7 +180,8 @@
 
 
 def factor_kernel(
-    place_ref, core_ref, mine_ref, other_ref, c0_ref, c1_ref, c2_ref, c3_ref, scores_ref, factor_ref, packed, work, inv
+    core_ref, mine_ref, other_ref, c0_ref, c1_ref, c2_ref, c3_ref, scores_ref, factor_ref,
+    packed, work, inv, whole, made, sems,
 ):
     lane = lax.broadcasted_iota(jnp.int32, (256, 256), 1)
     row = lax.broadcasted_iota(jnp.int32, (256, 256), 0)
@@ -263,23 +264,31 @@
                 ref[128 + low : 256 + low, col : col + 128] -= change[:, 128 * t : 128 * t + 128]
 
     upper = row[:128, :128] <= lane[:128, :128]
-    factor_ref[:128, :128] = jnp.where(upper, work[:128, :], 0.0)
-    factor_ref[:128, 128:] = work[128:256, :]
-    factor_ref[128:, :128] = jnp.zeros((128, 128), F32)
-    factor_ref[128:, 128:] = jnp.where(upper, work[256:, :], 0.0)
+    whole[:128, :128] = jnp.where(upper, work[:128, :], 0.0)
+    whole[:128, 128:] = work[128:256, :]
+    whole[128:, :128] = jnp.zeros((128, 128), F32)
+    whole[128:, 128:] = jnp.where(upper, work[256:, :], 0.0)
+    copies = [pltpu.make_async_copy(whole, factor_ref, sems.at[4])]
+    copies[0].start()
     high, middle, _ = three_terms(inv[...])
     right = jnp.concatenate([high, middle, high], axis=1)
-    place = place_ref[0]
+    place = lax.axis_index("x")
     for shift, coeffs in enumerate((c0_ref, c1_ref, c2_ref, c3_ref)):
-        first = pl.multiple_of(lax.rem(place + shift, 4) * PIECE, 16)
         high, middle, _ = three_terms(coeffs[...])
         left_side = jnp.concatenate([high, high, middle], axis=1)
-        scores_ref[pl.ds(first, PIECE), :] = lax.dot_general(
+        made[shift] = lax.dot_general(
             left_side, right, (((1,), (1,)), ((), ())), preferred_element_type=F32
         )
-
-
-def factor_and_scores(place, core, halves, pieces):
+        first = pl.multiple_of(lax.rem(place + shift, 4) * PIECE, 16)
+        copies.append(
+            pltpu.make_async_copy(made.at[shift], scores_ref.at[pl.ds(first, PIECE), :], sems.at[shift])
+        )
+        copies[-1].start()
+    for copy in copies:
+        copy.wait()
+
+
+def factor_and_scores(core, halves, pieces):
     vmem = pl.BlockSpec(memory_space=pltpu.VMEM)
     return pl.pallas_call(
         factor_kernel,
@@ -287,16 +296,19 @@
             jax.ShapeDtypeStruct((PART, PROBES), F32),
             jax.ShapeDtypeStruct((PROBES, PROBES), F32),
         ),
-        in_specs=[pl.BlockSpec(memory_space=pltpu.SMEM)] * 2 + [vmem] * 6,
-        out_specs=(vmem, vmem),
+        in_specs=[pl.BlockSpec(memory_space=pltpu.SMEM)] + [vmem] * 6,
+        out_specs=(pl.BlockSpec(memory_space=pl.ANY),) * 2,
         scratch_shapes=[
             pltpu.VMEM((2 * HALF, 128), F32),
             pltpu.VMEM((384, 128), F32),
             pltpu.VMEM((PROBES, PROBES), F32),
+            pltpu.VMEM((PROBES, PROBES), F32),
+            pltpu.VMEM((4, PIECE, PROBES), F32),
+            pltpu.SemaphoreType.DMA((5,)),
         ],
         compiler_params=pltpu.CompilerParams(vmem_limit_bytes=12 * 1024 * 1024),
         name="factor",
-    )(place, core, *halves, *pieces)
+    )(core, *halves, *pieces)
 
 
 def shifted(value, shift):
@@ -340,7 +352,6 @@
 
 
 def body(images, panels, mean_panels, ctf_table, pose_bin, ctf_group):
-    place = lax.axis_index("x").astype(jnp.int32).reshape(1)
     core = lax.axis_index("core").astype(jnp.int32).reshape(1)
     particles = PART * 64
     own, following, across, before = project(
@@ -351,7 +362,7 @@
     before = shifted(before, 3)
     coeffs, mine, other = gram_of(core, (kept(own), following, across, before), particles)
     halves, pieces = sum_everywhere(mine, other, coeffs)
-    return factor_and_scores(place, core, halves, (coeffs, *pieces))
+    return factor_and_scores(core, halves, (coeffs, *pieces))
 
 
 def solution(mesh):

time: 71.8 us -> 71.9 us (level)
  no operation moved by 1% of the time
where the time goes in v5:
time: 71.9 us; the launch traced here: 71.8 us
  starting transfers between devices  35.1 us (49%)
  Pallas kernels  18.3 us (25%)
  waiting for transfers between devices  16.6 us (23%)
  local copies, waits for them, and re-layouts  0.9 us (1%)
  between operations  0.88 us (1%)
    ppermute x7, starting transfers between devices, exchanged(): return lax.ppermute(value, ('z', 'y', 'core', 'x'), moves)  16.4 us
    ppermute x7, waiting for transfers between devices, exchanged(): return lax.ppermute(value, ('z', 'y', 'core', 'x'), moves)  11.6 us
    ppermute x2, starting transfers between devices, other_core(): return lax.ppermute(value, 'core', [(0, 1), (1, 0)])  10.3 us
    pallas_call x1, Pallas kernels, factor_and_scores(): pl.pallas_call(factor_kernel, out_shape=(jax.ShapeDtypeStruct((PART, PROB...  9.09 us
    pallas_call x1, Pallas kernels, project(): pl.pallas_call(project_kernel, out_shape=(piece,) * 4, in_specs=[anywhere...  8.79 us
    ppermute x6, starting transfers between devices, shifted(): return lax.ppermute(value, 'x', [(i, (i + shift) % 4) for i in range(4)])  8.38 us
    ppermute x6, waiting for transfers between devices, shifted(): return lax.ppermute(value, 'x', [(i, (i + shift) % 4) for i in range(4)])  3.15 us
    ppermute x2, waiting for transfers between devices, other_core(): return lax.ppermute(value, 'core', [(0, 1), (1, 0)])  1.81 us
  transfers between devices with their start and end apart: 15, of which 9 were waited for; matrix products, arithmetic and copies ran while one was open for 0% of the time, Pallas kernels for 0%

profile of v5, /device:TPU:1, one launch (start us, length us, event | category | flops | bytes accessed | tf_op | source)
XLA Modules:
  0.0 71.8 jit_solution(9703038628099307408)
XLA Ops:
  0.6 8.8 %project.1 = (f32[112,256]{1,0:T(8,128)}, f32[112,256]{1,0:T(8,128)}, f32[112,256]{1,0:T(8,128)}, f32[112,256]{1,0:T(8,128)}) custom-call(s32[1,448]{1,0:T(1,128)} %bitcast.3, s32[1,448]{1,0:T(1,128)} %bitcast.4, bf16[448,6400]{1,0:T(8,128)(2,1)} %images_ref.1, bf16[2,6400,256]{2,1,0:T(8,128)(2,1)} %panels_ref.1, f32[2,6400]{1,0:T(2,128)} %mean_ref.1, ...), custom_call_target="tpu_custom_call" | custom-call | tf_op jit(solution)/shard_map/project/pallas_call | solution.py:102
  9.4 2.1 %collective-permute-start = (f32[112,256]{1,0:T(8,128)}, f32[112,256]{1,0:T(8,128)S(1)}, u32[]{:S(2)}, u32[]{:S(2)}) collective-permute-start(f32[112,256]{1,0:T(8,128)} %get-tuple-element.16), channel_id=1, source_target_pairs={{0,1},{1,2},{2,3},{3,0},{4,5},{5,6},{6,7},{7,4},{8,9},{9,10},{10,1... | collective-permute-start | bytes 344072 | tf_op jit(solution)/shard_map/ppermute | solution.py:315
  11.6 2.5 %collective-permute-start.1 = (f32[112,256]{1,0:T(8,128)}, f32[112,256]{1,0:T(8,128)S(1)}, u32[]{:S(2)}, u32[]{:S(2)}) collective-permute-start(f32[112,256]{1,0:T(8,128)} %get-tuple-element.17), channel_id=1, source_target_pairs={{0,2},{1,3},{2,0},{3,1},{4,6},{5,7},{6,4},{7,5},{8,10},{9,11},{10,... | collective-permute-start | bytes 344072 | tf_op jit(solution)/shard_map/ppermute | solution.py:315
  14.0 1.2 %collective-permute-start.2 = (f32[112,256]{1,0:T(8,128)}, f32[112,256]{1,0:T(8,128)S(1)}, u32[]{:S(2)}, u32[]{:S(2)}) collective-permute-start(f32[112,256]{1,0:T(8,128)} %get-tuple-element.18), channel_id=1, source_target_pairs={{0,3},{1,0},{2,1},{3,2},{4,7},{5,4},{6,5},{7,6},{8,11},{9,8},{10,9... | collective-permute-start | bytes 344072 | tf_op jit(solution)/shard_map/ppermute | solution.py:315
  16.1 3.1 %collective-permute-done.1.second_ref = f32[112,256]{1,0:T(8,128)S(1)} collective-permute-done((f32[112,256]{1,0:T(8,128)}, f32[112,256]{1,0:T(8,128)S(1)}, u32[]{:S(2)}, u32[]{:S(2)}) %collective-permute-start.1) | collective-permute-done | bytes 114720 | tf_op jit(solution)/shard_map/ppermute | solution.py:315
  19.6 2.0 %collective-permute-start.3 = (f32[136,128]{1,0:T(8,128)S(1)}, f32[136,128]{1,0:T(8,128)S(1)}, u32[]{:S(2)}, u32[]{:S(2)}) collective-permute-start(f32[136,128]{1,0:T(8,128)S(1)} %get-tuple-element.20), channel_id=1, source_target_pairs={{0,4},{4,0},{1,5},{5,1},{2,6},{6,2},{3,7},{7,3},{8,12},{12,8},{9,1... | collective-permute-start | bytes 208904 | tf_op jit(solution)/shard_map/ppermute | solution.py:338
  21.6 0.9 %collective-permute-done.3 = f32[136,128]{1,0:T(8,128)S(1)} collective-permute-done((f32[136,128]{1,0:T(8,128)S(1)}, f32[136,128]{1,0:T(8,128)S(1)}, u32[]{:S(2)}, u32[]{:S(2)}) %collective-permute-start.3) | collective-permute-done | bytes 69664 | tf_op jit(solution)/shard_map/ppermute | solution.py:338
  22.5 1.0 %collective-permute-start.4 = (f32[136,128]{1,0:T(8,128)S(1)}, f32[136,128]{1,0:T(8,128)S(1)}, u32[]{:S(2)}, u32[]{:S(2)}) collective-permute-start(f32[136,128]{1,0:T(8,128)S(1)} %add.24), channel_id=1, source_target_pairs={{0,1},{1,0},{2,3},{3,2},{4,12},{5,13},{6,14},{7,15},{8,9},{9,8},{1... | collective-permute-start | bytes 208904 | tf_op jit(solution)/shard_map/ppermute | solution.py:334
  23.6 2.2 %collective-permute-done.4 = f32[136,128]{1,0:T(8,128)S(1)} collective-permute-done((f32[136,128]{1,0:T(8,128)S(1)}, f32[136,128]{1,0:T(8,128)S(1)}, u32[]{:S(2)}, u32[]{:S(2)}) %collective-permute-start.4) | collective-permute-done | bytes 69664 | tf_op jit(solution)/shard_map/ppermute | solution.py:334
  25.8 2.5 %collective-permute-start.5 = (f32[136,128]{1,0:T(8,128)S(1)}, f32[136,128]{1,0:T(8,128)S(1)}, u32[]{:S(2)}, u32[]{:S(2)}) collective-permute-start(f32[136,128]{1,0:T(8,128)S(1)} %add.25), channel_id=1, source_target_pairs={{0,3},{1,2},{2,1},{3,0},{4,28},{5,29},{6,30},{7,31},{8,11},{9,10},... | collective-permute-start | bytes 208904 | tf_op jit(solution)/shard_map/ppermute | solution.py:334
  28.3 2.0 %collective-permute-done.5 = f32[136,128]{1,0:T(8,128)S(1)} collective-permute-done((f32[136,128]{1,0:T(8,128)S(1)}, f32[136,128]{1,0:T(8,128)S(1)}, u32[]{:S(2)}, u32[]{:S(2)}) %collective-permute-start.5) | collective-permute-done | bytes 69664 | tf_op jit(solution)/shard_map/ppermute | solution.py:334
  30.3 1.1 %collective-permute-start.6 = (f32[136,128]{1,0:T(8,128)S(1)}, f32[136,128]{1,0:T(8,128)S(1)}, u32[]{:S(2)}, u32[]{:S(2)}) collective-permute-start(f32[136,128]{1,0:T(8,128)S(1)} %add.26), channel_id=1, source_target_pairs={{0,8},{1,9},{2,10},{3,11},{4,5},{5,4},{6,7},{7,6},{8,0},{9,1},{10,... | collective-permute-start | bytes 208904 | tf_op jit(solution)/shard_map/ppermute | solution.py:334
  31.4 2.1 %collective-permute-done.6 = f32[136,128]{1,0:T(8,128)S(1)} collective-permute-done((f32[136,128]{1,0:T(8,128)S(1)}, f32[136,128]{1,0:T(8,128)S(1)}, u32[]{:S(2)}, u32[]{:S(2)}) %collective-permute-start.6) | collective-permute-done | bytes 69664 | tf_op jit(solution)/shard_map/ppermute | solution.py:334
  33.5 2.4 %collective-permute-start.7 = (f32[136,128]{1,0:T(8,128)S(1)}, f32[136,128]{1,0:T(8,128)S(1)}, u32[]{:S(2)}, u32[]{:S(2)}) collective-permute-start(f32[136,128]{1,0:T(8,128)S(1)} %add.27), channel_id=1, source_target_pairs={{0,24},{1,25},{2,26},{3,27},{4,7},{5,6},{6,5},{7,4},{8,16},{9,17},... | collective-permute-start | bytes 208904 | tf_op jit(solution)/shard_map/ppermute | solution.py:334
  36.4 1.6 %collective-permute-done.7 = f32[136,128]{1,0:T(8,128)S(1)} collective-permute-done((f32[136,128]{1,0:T(8,128)S(1)}, f32[136,128]{1,0:T(8,128)S(1)}, u32[]{:S(2)}, u32[]{:S(2)}) %collective-permute-start.7) | collective-permute-done | bytes 69664 | tf_op jit(solution)/shard_map/ppermute | solution.py:334
  38.0 1.4 %collective-permute-start.8 = (f32[136,128]{1,0:T(8,128)S(1)}, f32[136,128]{1,0:T(8,128)S(1)}, u32[]{:S(2)}, u32[]{:S(2)}) collective-permute-start(f32[136,128]{1,0:T(8,128)S(1)} %add.28), channel_id=1, source_target_pairs={{0,32},{1,33},{2,34},{3,35},{4,36},{5,37},{6,38},{7,39},{8,40},{9,... | collective-permute-start | bytes 208904 | tf_op jit(solution)/shard_map/ppermute | solution.py:334
  39.4 2.2 %collective-permute-start.11 = (f32[112,256]{1,0:T(8,128)S(1)}, f32[112,256]{1,0:T(8,128)S(1)}, u32[]{:S(2)}, u32[]{:S(2)}) collective-permute-start(f32[112,256]{1,0:T(8,128)S(1)} %get-tuple-element.21.c0_ref), channel_id=1, source_target_pairs={{0,3},{1,0},{2,1},{3,2},{4,7},{5,4},{6,5},{7,6},{8,11},{9,8},{10,9... | collective-permute-start | bytes 344072 | tf_op jit(solution)/shard_map/ppermute | solution.py:315
  41.6 3.1 %collective-permute-start.10 = (f32[136,128]{1,0:T(8,128)S(1)}, f32[136,128]{1,0:T(8,128)S(1)}, u32[]{:S(2)}, u32[]{:S(2)}) collective-permute-start(f32[136,128]{1,0:T(8,128)S(1)} %add.29), channel_id=1, source_target_pairs={{0,64},{1,65},{2,66},{3,67},{4,68},{5,69},{6,70},{7,71},{8,72},{9,... | collective-permute-start | bytes 208904 | tf_op jit(solution)/shard_map/ppermute | solution.py:334
  44.7 1.9 %collective-permute-done.10 = f32[136,128]{1,0:T(8,128)S(1)} collective-permute-done((f32[136,128]{1,0:T(8,128)S(1)}, f32[136,128]{1,0:T(8,128)S(1)}, u32[]{:S(2)}, u32[]{:S(2)}) %collective-permute-start.10) | collective-permute-done | bytes 69664 | tf_op jit(solution)/shard_map/ppermute | solution.py:334
  46.6 4.9 %collective-permute-start.12 = (f32[136,128]{1,0:T(8,128)S(1)}, f32[136,128]{1,0:T(8,128)S(1)}, u32[]{:S(2)}, u32[]{:S(2)}) collective-permute-start(f32[136,128]{1,0:T(8,128)S(1)} %add.30), channel_id=1, source_target_pairs={{0,192},{1,193},{2,194},{3,195},{4,196},{5,197},{6,198},{7,199},{8... | collective-permute-start | bytes 208904 | tf_op jit(solution)/shard_map/ppermute | solution.py:334
  51.5 1.8 %collective-permute-done.12 = f32[136,128]{1,0:T(8,128)S(1)} collective-permute-done((f32[136,128]{1,0:T(8,128)S(1)}, f32[136,128]{1,0:T(8,128)S(1)}, u32[]{:S(2)}, u32[]{:S(2)}) %collective-permute-start.12) | collective-permute-done | bytes 69664 | tf_op jit(solution)/shard_map/ppermute | solution.py:334
  53.3 8.3 %collective-permute-start.14 = (f32[136,128]{1,0:T(8,128)S(1)}, f32[136,128]{1,0:T(8,128)S(1)}, u32[]{:S(2)}, u32[]{:S(2)}) collective-permute-start(f32[136,128]{1,0:T(8,128)S(1)} %add.31.mine_ref), channel_id=1, source_target_pairs={{0,4},{4,0},{1,5},{5,1},{2,6},{6,2},{3,7},{7,3},{8,12},{12,8},{9,1... | collective-permute-start | bytes 208904 | tf_op jit(solution)/shard_map/ppermute | solution.py:338
  61.7 0.9 %collective-permute-done.14.other_ref = f32[136,128]{1,0:T(8,128)S(1)} collective-permute-done((f32[136,128]{1,0:T(8,128)S(1)}, f32[136,128]{1,0:T(8,128)S(1)}, u32[]{:S(2)}, u32[]{:S(2)}) %collective-permute-start.14) | collective-permute-done | bytes 69664 | tf_op jit(solution)/shard_map/ppermute | solution.py:338
  62.6 9.1 %factor.1 = (f32[448,256]{1,0:T(8,128)}, f32[256,256]{1,0:T(8,128)}) custom-call(s32[1]{0:T(128)} %bitcast.core_ref, f32[136,128]{1,0:T(8,128)S(1)} %add.31.mine_ref, f32[136,128]{1,0:T(8,128)S(1)} %collective-permute-done.14.other_ref, f32[112,256]{1,0:T(8,128)S(1)} %get-tuple-element.21.c0_ref, f32[112,256]{1,0:T(8,128)S(1)} %collective-permute-done.11.c1_ref, ...), custom_call_target="tpu_custom_call" | custom-call | tf_op jit(solution)/shard_map/factor/pallas_call | solution.py:293
  (20 shorter events, 1.9 us)
Async XLA Ops:
  9.4 6.6 %collective-permute-start = (f32[112,256]{1,0:T(8,128)}, f32[112,256]{1,0:T(8,128)S(1)}, u32[]{:S(2)}, u32[]{:S(2)}) collective-permute-start(f32[112,256]{1,0:T(8,128)} %get-tuple-element.16), channel_id=1, source_target_pairs={{0,1},{1,2},{2,3},{3,0},{4,5},{5,6},{6,7},{7,4},{8,9},{9,10},{10,1... | collective-permute-start | bytes 344072 | tf_op jit(solution)/shard_map/ppermute | solution.py:315
  11.6 7.7 %collective-permute-start.1 = (f32[112,256]{1,0:T(8,128)}, f32[112,256]{1,0:T(8,128)S(1)}, u32[]{:S(2)}, u32[]{:S(2)}) collective-permute-start(f32[112,256]{1,0:T(8,128)} %get-tuple-element.17), channel_id=1, source_target_pairs={{0,2},{1,3},{2,0},{3,1},{4,6},{5,7},{6,4},{7,5},{8,10},{9,11},{10,... | collective-permute-start | bytes 344072 | tf_op jit(solution)/shard_map/ppermute | solution.py:315
  14.0 5.2 %collective-permute-start.2 = (f32[112,256]{1,0:T(8,128)}, f32[112,256]{1,0:T(8,128)S(1)}, u32[]{:S(2)}, u32[]{:S(2)}) collective-permute-start(f32[112,256]{1,0:T(8,128)} %get-tuple-element.18), channel_id=1, source_target_pairs={{0,3},{1,0},{2,1},{3,2},{4,7},{5,4},{6,5},{7,6},{8,11},{9,8},{10,9... | collective-permute-start | bytes 344072 | tf_op jit(solution)/shard_map/ppermute | solution.py:315
  15.2 0.9 %copy-start = (f32[112,256]{1,0:T(8,128)S(1)}, f32[112,256]{1,0:T(8,128)}, u32[]{:S(2)}) copy-start(f32[112,256]{1,0:T(8,128)} %get-tuple-element.15.piece_ref) | copy-start | bytes 344068
  19.6 2.9 %collective-permute-start.3 = (f32[136,128]{1,0:T(8,128)S(1)}, f32[136,128]{1,0:T(8,128)S(1)}, u32[]{:S(2)}, u32[]{:S(2)}) collective-permute-start(f32[136,128]{1,0:T(8,128)S(1)} %get-tuple-element.20), channel_id=1, source_target_pairs={{0,4},{4,0},{1,5},{5,1},{2,6},{6,2},{3,7},{7,3},{8,12},{12,8},{9,1... | collective-permute-start | bytes 208904 | tf_op jit(solution)/shard_map/ppermute | solution.py:338
  22.5 3.2 %collective-permute-start.4 = (f32[136,128]{1,0:T(8,128)S(1)}, f32[136,128]{1,0:T(8,128)S(1)}, u32[]{:S(2)}, u32[]{:S(2)}) collective-permute-start(f32[136,128]{1,0:T(8,128)S(1)} %add.24), channel_id=1, source_target_pairs={{0,1},{1,0},{2,3},{3,2},{4,12},{5,13},{6,14},{7,15},{8,9},{9,8},{1... | collective-permute-start | bytes 208904 | tf_op jit(solution)/shard_map/ppermute | solution.py:334
  25.8 4.5 %collective-permute-start.5 = (f32[136,128]{1,0:T(8,128)S(1)}, f32[136,128]{1,0:T(8,128)S(1)}, u32[]{:S(2)}, u32[]{:S(2)}) collective-permute-start(f32[136,128]{1,0:T(8,128)S(1)} %add.25), channel_id=1, source_target_pairs={{0,3},{1,2},{2,1},{3,0},{4,28},{5,29},{6,30},{7,31},{8,11},{9,10},... | collective-permute-start | bytes 208904 | tf_op jit(solution)/shard_map/ppermute | solution.py:334
  30.3 3.2 %collective-permute-start.6 = (f32[136,128]{1,0:T(8,128)S(1)}, f32[136,128]{1,0:T(8,128)S(1)}, u32[]{:S(2)}, u32[]{:S(2)}) collective-permute-start(f32[136,128]{1,0:T(8,128)S(1)} %add.26), channel_id=1, source_target_pairs={{0,8},{1,9},{2,10},{3,11},{4,5},{5,4},{6,7},{7,6},{8,0},{9,1},{10,... | collective-permute-start | bytes 208904 | tf_op jit(solution)/shard_map/ppermute | solution.py:334
  33.5 4.5 %collective-permute-start.7 = (f32[136,128]{1,0:T(8,128)S(1)}, f32[136,128]{1,0:T(8,128)S(1)}, u32[]{:S(2)}, u32[]{:S(2)}) collective-permute-start(f32[136,128]{1,0:T(8,128)S(1)} %add.27), channel_id=1, source_target_pairs={{0,24},{1,25},{2,26},{3,27},{4,7},{5,6},{6,5},{7,4},{8,16},{9,17},... | collective-permute-start | bytes 208904 | tf_op jit(solution)/shard_map/ppermute | solution.py:334
  35.9 5.7 %collective-permute-start.9 = (f32[112,256]{1,0:T(8,128)S(1)}, f32[112,256]{1,0:T(8,128)S(1)}, u32[]{:S(2)}, u32[]{:S(2)}) collective-permute-start(f32[112,256]{1,0:T(8,128)S(1)} %get-tuple-element.21.c0_ref), channel_id=1, source_target_pairs={{0,2},{1,3},{2,0},{3,1},{4,6},{5,7},{6,4},{7,5},{8,10},{9,11},{10,... | collective-permute-start | bytes 344072 | tf_op jit(solution)/shard_map/ppermute | solution.py:315
  38.0 3.6 %collective-permute-start.8 = (f32[136,128]{1,0:T(8,128)S(1)}, f32[136,128]{1,0:T(8,128)S(1)}, u32[]{:S(2)}, u32[]{:S(2)}) collective-permute-start(f32[136,128]{1,0:T(8,128)S(1)} %add.28), channel_id=1, source_target_pairs={{0,32},{1,33},{2,34},{3,35},{4,36},{5,37},{6,38},{7,39},{8,40},{9,... | collective-permute-start | bytes 208904 | tf_op jit(solution)/shard_map/ppermute | solution.py:334
  39.4 7.2 %collective-permute-start.11 = (f32[112,256]{1,0:T(8,128)S(1)}, f32[112,256]{1,0:T(8,128)S(1)}, u32[]{:S(2)}, u32[]{:S(2)}) collective-permute-start(f32[112,256]{1,0:T(8,128)S(1)} %get-tuple-element.21.c0_ref), channel_id=1, source_target_pairs={{0,3},{1,0},{2,1},{3,2},{4,7},{5,4},{6,5},{7,6},{8,11},{9,8},{10,9... | collective-permute-start | bytes 344072 | tf_op jit(solution)/shard_map/ppermute | solution.py:315
  41.6 5.0 %collective-permute-start.10 = (f32[136,128]{1,0:T(8,128)S(1)}, f32[136,128]{1,0:T(8,128)S(1)}, u32[]{:S(2)}, u32[]{:S(2)}) collective-permute-start(f32[136,128]{1,0:T(8,128)S(1)} %add.29), channel_id=1, source_target_pairs={{0,64},{1,65},{2,66},{3,67},{4,68},{5,69},{6,70},{7,71},{8,72},{9,... | collective-permute-start | bytes 208904 | tf_op jit(solution)/shard_map/ppermute | solution.py:334
  44.7 8.6 %collective-permute-start.13 = (f32[112,256]{1,0:T(8,128)S(1)}, f32[112,256]{1,0:T(8,128)S(1)}, u32[]{:S(2)}, u32[]{:S(2)}) collective-permute-start(f32[112,256]{1,0:T(8,128)S(1)} %get-tuple-element.21.c0_ref), channel_id=1, source_target_pairs={{0,1},{1,2},{2,3},{3,0},{4,5},{5,6},{6,7},{7,4},{8,9},{9,10},{10,1... | collective-permute-start | bytes 344072 | tf_op jit(solution)/shard_map/ppermute | solution.py:315
  46.6 6.7 %collective-permute-start.12 = (f32[136,128]{1,0:T(8,128)S(1)}, f32[136,128]{1,0:T(8,128)S(1)}, u32[]{:S(2)}, u32[]{:S(2)}) collective-permute-start(f32[136,128]{1,0:T(8,128)S(1)} %add.30), channel_id=1, source_target_pairs={{0,192},{1,193},{2,194},{3,195},{4,196},{5,197},{6,198},{7,199},{8... | collective-permute-start | bytes 208904 | tf_op jit(solution)/shard_map/ppermute | solution.py:334
  53.3 9.2 %collective-permute-start.14 = (f32[136,128]{1,0:T(8,128)S(1)}, f32[136,128]{1,0:T(8,128)S(1)}, u32[]{:S(2)}, u32[]{:S(2)}) collective-permute-start(f32[136,128]{1,0:T(8,128)S(1)} %add.31.mine_ref), channel_id=1, source_target_pairs={{0,4},{4,0},{1,5},{5,1},{2,6},{6,2},{3,7},{7,3},{8,12},{12,8},{9,1... | collective-permute-start | bytes 208904 | tf_op jit(solution)/shard_map/ppermute | solution.py:338
